TPU v7x, 32 devices: a whole 2x2x4 slice. The times are simulated.
32 devices in a mesh: ka: 4 (over x, core), fit: 8 (over z, y).
Axes of the slice: x: 2, y: 2, z: 4, core: 2. Of those that a mesh axis runs over, the one named last changes fastest.
Arguments:
- integrals: bfloat16 [3, 4, 8, 48, 64, 128], P(None, 'ka', 'fit'), may hold values from -0.3125 to 0.3125
- block_lists: int32 [3, 4, 8, 2, 48], P(None, 'ka', 'fit'), may hold values from 0 to 15, as said below
- coeff: bfloat16 [4, 2, 1024, 256], P('ka', None, 'fit'), may hold values from -6 to 6
- match: int32 [3, 4], replicated, may hold values from 0 to 3, each once within a row
- ex_blocks: int32 [4, 2, 64], P('ka'), may hold values from 0 to 15, as said below
Outputs:
- exchange: float32 [4, 4096, 128], P('ka', 'fit')
Inputs may be any that keep to these rules, and one draw needn't show every extreme that they name: `block_lists`: each integral matrix lists 48 distinct blocks; each entry is a block index below 16, row first then column. `ex_blocks`: each k-point lists 64 distinct blocks, none on the diagonal (row block differs from column block).
All inputs are finite; a program needn't handle non-finite values.
Results may differ from a plain program's by a relative error of at most 0.0036.
Values may be sent and summed in bfloat16 or wider, within the bound.
No kernel may reach another device: no remote copies, remote signals or barrier semaphores. Data moves between devices by JAX's collectives and lax.ppermute only.
A program may use at most 128 MiB of HBM per device.

v0:
```python
import functools

import jax
import jax.numpy as jnp
from jax import lax
from jax.experimental import pallas as pl
from jax.experimental.pallas import tpu as pltpu
from jax.sharding import PartitionSpec as P

AXES = ("ka", "fit")


def bits_of(size):
    return [1 << b for b in range(size.bit_length() - 1)]


def gather_pieces(shard, nka, nfit):
    def swap(arr, dka, dfit):
        perm = [
            (k * nfit + f, (k ^ dka) * nfit + (f ^ dfit))
            for k in range(nka)
            for f in range(nfit)
        ]
        return lax.ppermute(arr, AXES, perm)

    core, xbit = 1, nka // 2
    fit_bits = bits_of(nfit)
    ybit, wbit = fit_bits[0], fit_bits[1]
    got = {}

    def send(key, dka, dfit):
        kind, ka, fit = key
        got[(kind, ka ^ dka, fit ^ dfit)] = swap(got[key], dka, dfit)

    x, y, w = (xbit, 0), (0, ybit), (0, wbit)
    a, b = ("near", 0, 0), ("far", 0, 0)

    def at(key, *steps):
        kind, ka, fit = key
        for dka, dfit in steps:
            ka, fit = ka ^ dka, fit ^ dfit
        return (kind, ka, fit)

    got[a] = shard
    stack = shard
    offsets = [0]
    for bit in fit_bits[2:]:
        stack = jnp.concatenate([stack, swap(stack, 0, bit)], axis=0) if bit != fit_bits[-1] or len(fit_bits) > 3 else None
        offsets = offsets + [o ^ bit for o in offsets]
    if stack is None:
        got[b] = swap(shard, 0, fit_bits[2])
    else:
        got[b] = stack[1:]
    send(a, *x)
    send(a, *y)
    send(a, *w)
    send(b, *x)
    send(at(a, w), *x)
    send(b, *y)
    send(at(a, x), *y)
    send(b, *w)
    send(at(a, y), *w)
    send(at(a, y, w), *x)
    send(at(b, y), *x)
    send(at(b, w), *y)
    send(at(b, x), *w)
    send(at(b, y, w), *x)
    for key in list(got):
        send(key, core, 0)
    return got, offsets[1:]


def exchange_kernel(
    keys, far, nq, nblk, nexch, edge, occ, nbl, match_ref, lists_ref, ex_ref, lmat_ref, *refs
):
    pieces = refs[: len(keys)]
    out_ref, ops_ref, sums_ref, x_ref = refs[len(keys) :]
    ka, fit = lax.axis_index("ka"), lax.axis_index("fit")
    rows = pieces[0].shape[2]
    sub = min(rows, edge)

    def one_q(qq, carry):
        want = lax.bitwise_xor(match_ref[qq, ka], ka)

        for dka in sorted({key[1] for key in keys}):

            @pl.when(want == dka)
            def _():
                for key, piece in zip(keys, pieces):
                    if key[1] != dka:
                        continue
                    offs = [key[2]] if key[0] == "near" else [key[2] ^ o for o in far]
                    for index, off in enumerate(offs):
                        owner = lax.bitwise_xor(fit, off)
                        for part in range(rows // sub):
                            row = owner * rows + part * sub
                            dst = (row // edge) * (2 * edge) + lax.rem(row, edge)
                            dst = pl.multiple_of(dst, sub)
                            real = piece[index, 0, part * sub : (part + 1) * sub, :]
                            imag = piece[index, 1, part * sub : (part + 1) * sub, :]
                            ops_ref[pl.ds(dst, sub), :occ] = real
                            ops_ref[pl.ds(dst, sub), occ:] = imag
                            low = pl.multiple_of(dst + edge, sub)
                            ops_ref[pl.ds(low, sub), :occ] = -imag
                            ops_ref[pl.ds(low, sub), occ:] = real

        sums_ref[...] = jnp.zeros_like(sums_ref)

        def one_block(n, c):
            rb = pl.multiple_of(lists_ref[qq, 0, 0, 0, n] * edge, edge)
            cb = pl.multiple_of(lists_ref[qq, 0, 0, 1, n] * (2 * edge), 2 * edge)
            sums_ref[pl.ds(rb, edge), :] += jnp.dot(
                lmat_ref[qq, 0, 0, n],
                ops_ref[pl.ds(cb, 2 * edge), :],
                preferred_element_type=jnp.float32,
            )
            return c

        lax.fori_loop(0, nblk, one_block, 0, unroll=4)

        for rb in range(nbl):
            x = sums_ref[rb * edge : (rb + 1) * edge, :].astype(jnp.bfloat16)
            x_ref[qq, rb, :edge, :] = x
            x_ref[qq, rb, edge:, :occ] = -x[:, occ:]
            x_ref[qq, rb, edge:, occ:] = x[:, :occ]
        return carry

    lax.fori_loop(0, nq, one_q, 0)

    def one_pair(e, c):
        left, right = ex_ref[0, 0, e], ex_ref[0, 1, e]
        acc = None
        for qq in range(nq):
            term = lax.dot_general(
                x_ref[qq, left, :edge, :],
                x_ref[qq, right],
                (((1,), (1,)), ((), ())),
                preferred_element_type=jnp.float32,
            )
            acc = term if acc is None else acc + term
        out_ref[pl.ds(pl.multiple_of(e * edge, edge), edge), :] = acc.astype(out_ref.dtype)
        return c

    lax.fori_loop(0, nexch, one_pair, 0, unroll=4)


def on_device(nka, nfit, integrals, block_lists, coeff, match, ex_blocks):
    nq, _, _, nblk, edge, _ = integrals.shape
    occ = coeff.shape[3]
    nexch = ex_blocks.shape[2]
    nbl = nfit * coeff.shape[2] // edge
    got, far = gather_pieces(coeff, nka, nfit)
    keys = sorted(got)
    vmem = pl.BlockSpec(memory_space=pltpu.VMEM)
    smem = pl.BlockSpec(memory_space=pltpu.SMEM)
    partial = pl.pallas_call(
        functools.partial(exchange_kernel, keys, far, nq, nblk, nexch, edge, occ, nbl),
        out_shape=jax.ShapeDtypeStruct((nexch * edge, 2 * edge), jnp.bfloat16),
        in_specs=[smem, smem, smem, vmem] + [vmem] * len(keys),
        out_specs=vmem,
        scratch_shapes=[
            pltpu.VMEM((nbl * 2 * edge, 2 * occ), jnp.bfloat16),
            pltpu.VMEM((nbl * edge, 2 * occ), jnp.float32),
            pltpu.VMEM((nq, nbl, 2 * edge, 2 * occ), jnp.bfloat16),
        ],
        compiler_params=pltpu.CompilerParams(vmem_limit_bytes=48 * 1024 * 1024),
    )(match, block_lists, ex_blocks, integrals, *[got[key] for key in keys])
    spread = lax.all_to_all(partial, "fit", 0, 0, tiled=True)
    factor = -((nq * nfit * occ) ** (-0.5))
    parts = spread.reshape(nfit, nexch * edge // nfit, 2 * edge).astype(jnp.float32)
    return (jnp.sum(parts, axis=0) * factor)[None]


def solution(mesh):
    nka, nfit = mesh.shape["ka"], mesh.shape["fit"]
    return jax.shard_map(
        functools.partial(on_device, nka, nfit),
        mesh=mesh,
        in_specs=(
            P(None, "ka", "fit", None, None, None),
            P(None, "ka", "fit", None, None),
            P("ka", None, "fit", None),
            P(),
            P("ka", None, None),
        ),
        out_specs=P("ka", "fit", None),
        check_vma=False,
    )
```

profile of v0, /device:TPU:0, one launch (start us, length us, event | category | flops | bytes accessed | tf_op | source)
XLA Modules:
  0.0 93.3 jit_solution(16603134037946106449)
XLA Ops:
  0.0 3.0 %collective-permute-start.17 = (bf16[1,2,128,256]{3,2,1,0:T(8,128)(2,1)}, bf16[1,2,128,256]{3,2,1,0:T(8,128)(2,1)S(1)}, u32[]{:S(2)}, u32[]{:S(2)}) collective-permute-start(bf16[1,2,128,256]{3,2,1,0:T(8,128)(2,1)} %refs_16_.1), channel_id=1, source_target_pairs={{0,2},{1,3},{2,0},{3,1},{4,6},{5,7},{6,4},{7,5},{8,10},{9,11},{10,... | collective-permute-start | bytes 393224 | tf_op jit(solution)/shard_map/ppermute | solution.py:24
  3.0 0.0 collective-permute-start.19
  3.0 1.5 %collective-permute-start.16 = (bf16[1,2,128,256]{3,2,1,0:T(8,128)(2,1)}, bf16[1,2,128,256]{3,2,1,0:T(8,128)(2,1)S(1)}, u32[]{:S(2)}, u32[]{:S(2)}) collective-permute-start(bf16[1,2,128,256]{3,2,1,0:T(8,128)(2,1)} %refs_16_.1), channel_id=1, source_target_pairs={{0,1},{1,0},{2,3},{3,2},{4,5},{5,4},{6,7},{7,6},{8,9},{9,8},{10,11... | collective-permute-start | bytes 393224 | tf_op jit(solution)/shard_map/ppermute | solution.py:24
  4.5 2.6 %collective-permute-start = (bf16[1,2,128,256]{3,2,1,0:T(8,128)(2,1)}, bf16[1,2,128,256]{3,2,1,0:T(8,128)(2,1)S(1)}, u32[]{:S(2)}, u32[]{:S(2)}) collective-permute-start(bf16[1,2,128,256]{3,2,1,0:T(8,128)(2,1)} %refs_16_.1), channel_id=1, source_target_pairs={{0,4},{1,5},{2,6},{3,7},{4,0},{5,1},{6,2},{7,3},{8,12},{9,13},{10,... | collective-permute-start | bytes 393224 | tf_op jit(solution)/shard_map/ppermute | solution.py:24
  7.1 1.5 %collective-permute-start.23 = (bf16[1,2,128,256]{3,2,1,0:T(8,128)(2,1)}, bf16[1,2,128,256]{3,2,1,0:T(8,128)(2,1)S(1)}, u32[]{:S(2)}, u32[]{:S(2)}) collective-permute-start(bf16[1,2,128,256]{3,2,1,0:T(8,128)(2,1)} %refs_16_.1), channel_id=1, source_target_pairs={{0,16},{1,17},{2,18},{3,19},{4,20},{5,21},{6,22},{7,23},{8,24},{9,... | collective-permute-start | bytes 393224 | tf_op jit(solution)/shard_map/ppermute | solution.py:24
  8.6 0.5 collective-permute-start.25
  9.2 0.5 collective-permute-start.20
  9.7 4.4 %collective-permute-done.refs_0_ = bf16[1,2,128,256]{3,2,1,0:T(8,128)(2,1)S(1)} collective-permute-done((bf16[1,2,128,256]{3,2,1,0:T(8,128)(2,1)}, bf16[1,2,128,256]{3,2,1,0:T(8,128)(2,1)S(1)}, u32[]{:S(2)}, u32[]{:S(2)}) %collective-permute-start) | collective-permute-done | bytes 131104 | tf_op jit(solution)/shard_map/ppermute | solution.py:24
  14.1 0.0 collective-permute-start.18
  14.1 1.5 %collective-permute-start.8 = (bf16[1,2,128,256]{3,2,1,0:T(8,128)(2,1)S(1)}, bf16[1,2,128,256]{3,2,1,0:T(8,128)(2,1)S(1)}, u32[]{:S(2)}, u32[]{:S(2)}) collective-permute-start(bf16[1,2,128,256]{3,2,1,0:T(8,128)(2,1)S(1)} %collective-permute-done.refs_0_), channel_id=1, source_target_pairs={{0,16},{1,17},{2,18},{3,19},{4,20},{5,21},{6,22},{7,23},{8,24},{9,... | collective-permute-start | bytes 393224 | tf_op jit(solution)/shard_map/ppermute | solution.py:24
  15.6 0.0 collective-permute-done.21.refs_22_
  15.6 2.1 %collective-permute-start.2 = (bf16[1,2,128,256]{3,2,1,0:T(8,128)(2,1)S(1)}, bf16[1,2,128,256]{3,2,1,0:T(8,128)(2,1)S(1)}, u32[]{:S(2)}, u32[]{:S(2)}) collective-permute-start(bf16[1,2,128,256]{3,2,1,0:T(8,128)(2,1)S(1)} %collective-permute-done.refs_0_), channel_id=1, source_target_pairs={{0,2},{1,3},{2,0},{3,1},{4,6},{5,7},{6,4},{7,5},{8,10},{9,11},{10,... | collective-permute-start | bytes 393224 | tf_op jit(solution)/shard_map/ppermute | solution.py:24
  17.7 0.6 collective-permute-start.1
  18.2 1.3 %collective-permute-done.18.refs_19_ = bf16[1,2,128,256]{3,2,1,0:T(8,128)(2,1)S(1)} collective-permute-done((bf16[1,2,128,256]{3,2,1,0:T(8,128)(2,1)S(1)}, bf16[1,2,128,256]{3,2,1,0:T(8,128)(2,1)S(1)}, u32[]{:S(2)}, u32[]{:S(2)}) %collective-permute-start.18) | collective-permute-done | bytes 131104 | tf_op jit(solution)/shard_map/ppermute | solution.py:24
  19.5 0.0 collective-permute-start.27
  19.5 0.3 collective-permute-start.24
  19.8 0.3 collective-permute-start.29
  20.1 2.0 %collective-permute-done.2.refs_2_ = bf16[1,2,128,256]{3,2,1,0:T(8,128)(2,1)S(1)} collective-permute-done((bf16[1,2,128,256]{3,2,1,0:T(8,128)(2,1)S(1)}, bf16[1,2,128,256]{3,2,1,0:T(8,128)(2,1)S(1)}, u32[]{:S(2)}, u32[]{:S(2)}) %collective-permute-start.2) | collective-permute-done | bytes 131104 | tf_op jit(solution)/shard_map/ppermute | solution.py:24
  22.1 1.5 %collective-permute-start.26 = (bf16[1,2,128,256]{3,2,1,0:T(8,128)(2,1)S(1)}, bf16[1,2,128,256]{3,2,1,0:T(8,128)(2,1)S(1)}, u32[]{:S(2)}, u32[]{:S(2)}) collective-permute-start(bf16[1,2,128,256]{3,2,1,0:T(8,128)(2,1)S(1)} %collective-permute-done.18.refs_19_), channel_id=1, source_target_pairs={{0,16},{1,17},{2,18},{3,19},{4,20},{5,21},{6,22},{7,23},{8,24},{9,... | collective-permute-start | bytes 393224 | tf_op jit(solution)/shard_map/ppermute | solution.py:24
  23.6 0.2 collective-permute-done.1.refs_1_
  23.8 0.0 collective-permute-start.22
  23.8 0.5 collective-permute-start.12
  24.3 1.7 %collective-permute-done.24.refs_25_ = bf16[1,2,128,256]{3,2,1,0:T(8,128)(2,1)S(1)} collective-permute-done((bf16[1,2,128,256]{3,2,1,0:T(8,128)(2,1)S(1)}, bf16[1,2,128,256]{3,2,1,0:T(8,128)(2,1)S(1)}, u32[]{:S(2)}, u32[]{:S(2)}) %collective-permute-start.24) | collective-permute-done | bytes 131104 | tf_op jit(solution)/shard_map/ppermute | solution.py:24
  26.0 0.4 collective-permute-start.10
  26.4 0.6 collective-permute-start.3
  27.0 0.4 collective-permute-done.26.refs_27_
  27.3 1.2 %collective-permute-start.9 = (bf16[1,2,128,256]{3,2,1,0:T(8,128)(2,1)S(1)}, bf16[1,2,128,256]{3,2,1,0:T(8,128)(2,1)S(1)}, u32[]{:S(2)}, u32[]{:S(2)}) collective-permute-start(bf16[1,2,128,256]{3,2,1,0:T(8,128)(2,1)S(1)} %collective-permute-done.1.refs_1_), channel_id=1, source_target_pairs={{0,16},{1,17},{2,18},{3,19},{4,20},{5,21},{6,22},{7,23},{8,24},{9,... | collective-permute-start | bytes 393224 | tf_op jit(solution)/shard_map/ppermute | solution.py:24
  28.5 0.0 collective-permute-done.12.refs_12_
  28.5 0.2 collective-permute-start.5
  28.8 2.2 %collective-permute-done.10.refs_10_ = bf16[1,2,128,256]{3,2,1,0:T(8,128)(2,1)S(1)} collective-permute-done((bf16[1,2,128,256]{3,2,1,0:T(8,128)(2,1)S(1)}, bf16[1,2,128,256]{3,2,1,0:T(8,128)(2,1)S(1)}, u32[]{:S(2)}, u32[]{:S(2)}) %collective-permute-start.10) | collective-permute-done | bytes 131104 | tf_op jit(solution)/shard_map/ppermute | solution.py:24
  31.0 0.0 collective-permute-start.28
  31.0 0.4 collective-permute-done.3.refs_3_
  31.4 1.1 %collective-permute-start.11 = (bf16[1,2,128,256]{3,2,1,0:T(8,128)(2,1)S(1)}, bf16[1,2,128,256]{3,2,1,0:T(8,128)(2,1)S(1)}, u32[]{:S(2)}, u32[]{:S(2)}) collective-permute-start(bf16[1,2,128,256]{3,2,1,0:T(8,128)(2,1)S(1)} %collective-permute-done.3.refs_3_), channel_id=1, source_target_pairs={{0,16},{1,17},{2,18},{3,19},{4,20},{5,21},{6,22},{7,23},{8,24},{9,... | collective-permute-start | bytes 393224 | tf_op jit(solution)/shard_map/ppermute | solution.py:24
  32.5 0.2 collective-permute-start.7
  32.7 0.6 collective-permute-done.9.refs_9_
  33.2 0.5 collective-permute-start.14
  33.8 0.1 collective-permute-start.13
  33.8 3.1 %collective-permute-done.11.refs_11_ = bf16[1,2,128,256]{3,2,1,0:T(8,128)(2,1)S(1)} collective-permute-done((bf16[1,2,128,256]{3,2,1,0:T(8,128)(2,1)S(1)}, bf16[1,2,128,256]{3,2,1,0:T(8,128)(2,1)S(1)}, u32[]{:S(2)}, u32[]{:S(2)}) %collective-permute-start.11) | collective-permute-done | bytes 131104 | tf_op jit(solution)/shard_map/ppermute | solution.py:24
  36.9 0.0 collective-permute-start.15
  37.0 1.3 %collective-permute-done.15.refs_15_ = bf16[1,2,128,256]{3,2,1,0:T(8,128)(2,1)S(1)} collective-permute-done((bf16[1,2,128,256]{3,2,1,0:T(8,128)(2,1)S(1)}, bf16[1,2,128,256]{3,2,1,0:T(8,128)(2,1)S(1)}, u32[]{:S(2)}, u32[]{:S(2)}) %collective-permute-start.15) | collective-permute-done | bytes 131104 | tf_op jit(solution)/shard_map/ppermute | solution.py:24
  38.3 0.9 copy-done
  39.2 0.7 copy-done.1
  39.9 0.7 copy-done.2
  40.5 0.7 copy-done.3
  41.2 21.6 %shard_map.55 = bf16[4096,128]{1,0:T(8,128)(2,1)S(1)} custom-call(s32[3,4]{1,0:T(4,128)S(1)} %copy-done.2, s32[3,1,1,2,48]{4,3,2,1,0:T(2,128)S(1)} %copy-done.1, s32[1,2,64]{2,1,0:T(2,128)S(1)} %copy-done.3, bf16[3,1,1,48,64,128]{5,4,3,2,1,0:T(8,128)(2,1)} %lmat_ref.1, bf16[1,2,128,256]{3,2,1,0:T(8,128)(2,1)S(1)} %collective-permute-done.refs_0_, ...), custom_call_target="tpu_custom_call" | custom-call | tf_op jit(solution)/shard_map/pallas_call | solution.py:156
  62.8 29.6 %all_to_all.9 = bf16[8,512,128]{2,1,0:T(8,128)(2,1)S(1)} all-to-all(bf16[8,512,128]{2,1,0:T(8,128)(2,1)S(1)} %bitcast.3), channel_id=1, replica_groups=mesh['ka'=4,'fit'=8] {'fit'}, dimensions={0} | all-to-all | bytes 2097152 | tf_op jit(solution)/shard_map/all_to_all | solution.py:168
  92.5 0.1 convert_reduce_fusion
  92.6 0.7 multiply_bitcast_fusion
  (26 shorter events, 0.1 us)
Async XLA Ops:
  0.0 8.6 %collective-permute-start.17 = (bf16[1,2,128,256]{3,2,1,0:T(8,128)(2,1)}, bf16[1,2,128,256]{3,2,1,0:T(8,128)(2,1)S(1)}, u32[]{:S(2)}, u32[]{:S(2)}) collective-permute-start(bf16[1,2,128,256]{3,2,1,0:T(8,128)(2,1)} %refs_16_.1), channel_id=1, source_target_pairs={{0,2},{1,3},{2,0},{3,1},{4,6},{5,7},{6,4},{7,5},{8,10},{9,11},{10,... | collective-permute-start | bytes 393224 | tf_op jit(solution)/shard_map/ppermute | solution.py:24
  3.0 6.1 %collective-permute-start.19 = (bf16[1,2,128,256]{3,2,1,0:T(8,128)(2,1)}, bf16[1,2,128,256]{3,2,1,0:T(8,128)(2,1)S(1)}, u32[]{:S(2)}, u32[]{:S(2)}) collective-permute-start(bf16[1,2,128,256]{3,2,1,0:T(8,128)(2,1)} %refs_16_.1), channel_id=1, source_target_pairs={{0,8},{1,9},{2,10},{3,11},{4,12},{5,13},{6,14},{7,15},{8,0},{9,1},... | collective-permute-start | bytes 393224 | tf_op jit(solution)/shard_map/ppermute | solution.py:24
  3.0 6.1 %collective-permute-start.16 = (bf16[1,2,128,256]{3,2,1,0:T(8,128)(2,1)}, bf16[1,2,128,256]{3,2,1,0:T(8,128)(2,1)S(1)}, u32[]{:S(2)}, u32[]{:S(2)}) collective-permute-start(bf16[1,2,128,256]{3,2,1,0:T(8,128)(2,1)} %refs_16_.1), channel_id=1, source_target_pairs={{0,1},{1,0},{2,3},{3,2},{4,5},{5,4},{6,7},{7,6},{8,9},{9,8},{10,11... | collective-permute-start | bytes 393224 | tf_op jit(solution)/shard_map/ppermute | solution.py:24
  4.5 9.5 %collective-permute-start = (bf16[1,2,128,256]{3,2,1,0:T(8,128)(2,1)}, bf16[1,2,128,256]{3,2,1,0:T(8,128)(2,1)S(1)}, u32[]{:S(2)}, u32[]{:S(2)}) collective-permute-start(bf16[1,2,128,256]{3,2,1,0:T(8,128)(2,1)} %refs_16_.1), channel_id=1, source_target_pairs={{0,4},{1,5},{2,6},{3,7},{4,0},{5,1},{6,2},{7,3},{8,12},{9,13},{10,... | collective-permute-start | bytes 393224 | tf_op jit(solution)/shard_map/ppermute | solution.py:24
  7.1 6.9 %collective-permute-start.23 = (bf16[1,2,128,256]{3,2,1,0:T(8,128)(2,1)}, bf16[1,2,128,256]{3,2,1,0:T(8,128)(2,1)S(1)}, u32[]{:S(2)}, u32[]{:S(2)}) collective-permute-start(bf16[1,2,128,256]{3,2,1,0:T(8,128)(2,1)} %refs_16_.1), channel_id=1, source_target_pairs={{0,16},{1,17},{2,18},{3,19},{4,20},{5,21},{6,22},{7,23},{8,24},{9,... | collective-permute-start | bytes 393224 | tf_op jit(solution)/shard_map/ppermute | solution.py:24
  8.6 6.9 %collective-permute-start.25 = (bf16[1,2,128,256]{3,2,1,0:T(8,128)(2,1)S(1)}, bf16[1,2,128,256]{3,2,1,0:T(8,128)(2,1)S(1)}, u32[]{:S(2)}, u32[]{:S(2)}) collective-permute-start(bf16[1,2,128,256]{3,2,1,0:T(8,128)(2,1)S(1)} %collective-permute-done.17.refs_18_), channel_id=1, source_target_pairs={{0,16},{1,17},{2,18},{3,19},{4,20},{5,21},{6,22},{7,23},{8,24},{9,... | collective-permute-start | bytes 393224 | tf_op jit(solution)/shard_map/ppermute | solution.py:24
  9.2 6.4 %collective-permute-start.21 = (bf16[1,2,128,256]{3,2,1,0:T(8,128)(2,1)S(1)}, bf16[1,2,128,256]{3,2,1,0:T(8,128)(2,1)S(1)}, u32[]{:S(2)}, u32[]{:S(2)}) collective-permute-start(bf16[1,2,128,256]{3,2,1,0:T(8,128)(2,1)S(1)} %collective-permute-done.17.refs_18_), channel_id=1, source_target_pairs={{0,8},{1,9},{2,10},{3,11},{4,12},{5,13},{6,14},{7,15},{8,0},{9,1},... | collective-permute-start | bytes 393224 | tf_op jit(solution)/shard_map/ppermute | solution.py:24
  9.2 8.5 %collective-permute-start.20 = (bf16[1,2,128,256]{3,2,1,0:T(8,128)(2,1)S(1)}, bf16[1,2,128,256]{3,2,1,0:T(8,128)(2,1)S(1)}, u32[]{:S(2)}, u32[]{:S(2)}) collective-permute-start(bf16[1,2,128,256]{3,2,1,0:T(8,128)(2,1)S(1)} %collective-permute-done.16.refs_17_), channel_id=1, source_target_pairs={{0,8},{1,9},{2,10},{3,11},{4,12},{5,13},{6,14},{7,15},{8,0},{9,1},... | collective-permute-start | bytes 393224 | tf_op jit(solution)/shard_map/ppermute | solution.py:24
  14.1 5.4 %collective-permute-start.18 = (bf16[1,2,128,256]{3,2,1,0:T(8,128)(2,1)S(1)}, bf16[1,2,128,256]{3,2,1,0:T(8,128)(2,1)S(1)}, u32[]{:S(2)}, u32[]{:S(2)}) collective-permute-start(bf16[1,2,128,256]{3,2,1,0:T(8,128)(2,1)S(1)} %collective-permute-done.16.refs_17_), channel_id=1, source_target_pairs={{0,2},{1,3},{2,0},{3,1},{4,6},{5,7},{6,4},{7,5},{8,10},{9,11},{10,... | collective-permute-start | bytes 393224 | tf_op jit(solution)/shard_map/ppermute | solution.py:24
  14.1 5.4 %collective-permute-start.8 = (bf16[1,2,128,256]{3,2,1,0:T(8,128)(2,1)S(1)}, bf16[1,2,128,256]{3,2,1,0:T(8,128)(2,1)S(1)}, u32[]{:S(2)}, u32[]{:S(2)}) collective-permute-start(bf16[1,2,128,256]{3,2,1,0:T(8,128)(2,1)S(1)} %collective-permute-done.refs_0_), channel_id=1, source_target_pairs={{0,16},{1,17},{2,18},{3,19},{4,20},{5,21},{6,22},{7,23},{8,24},{9,... | collective-permute-start | bytes 393224 | tf_op jit(solution)/shard_map/ppermute | solution.py:24
  15.6 4.2 %collective-permute-start.4 = (bf16[1,2,128,256]{3,2,1,0:T(8,128)(2,1)S(1)}, bf16[1,2,128,256]{3,2,1,0:T(8,128)(2,1)S(1)}, u32[]{:S(2)}, u32[]{:S(2)}) collective-permute-start(bf16[1,2,128,256]{3,2,1,0:T(8,128)(2,1)S(1)} %collective-permute-done.refs_0_), channel_id=1, source_target_pairs={{0,8},{1,9},{2,10},{3,11},{4,12},{5,13},{6,14},{7,15},{8,0},{9,1},... | collective-permute-start | bytes 393224 | tf_op jit(solution)/shard_map/ppermute | solution.py:24
  15.6 6.5 %collective-permute-start.2 = (bf16[1,2,128,256]{3,2,1,0:T(8,128)(2,1)S(1)}, bf16[1,2,128,256]{3,2,1,0:T(8,128)(2,1)S(1)}, u32[]{:S(2)}, u32[]{:S(2)}) collective-permute-start(bf16[1,2,128,256]{3,2,1,0:T(8,128)(2,1)S(1)} %collective-permute-done.refs_0_), channel_id=1, source_target_pairs={{0,2},{1,3},{2,0},{3,1},{4,6},{5,7},{6,4},{7,5},{8,10},{9,11},{10,... | collective-permute-start | bytes 393224 | tf_op jit(solution)/shard_map/ppermute | solution.py:24
  17.7 6.1 %collective-permute-start.1 = (bf16[1,2,128,256]{3,2,1,0:T(8,128)(2,1)S(1)}, bf16[1,2,128,256]{3,2,1,0:T(8,128)(2,1)S(1)}, u32[]{:S(2)}, u32[]{:S(2)}) collective-permute-start(bf16[1,2,128,256]{3,2,1,0:T(8,128)(2,1)S(1)} %collective-permute-done.refs_0_), channel_id=1, source_target_pairs={{0,1},{1,0},{2,3},{3,2},{4,5},{5,4},{6,7},{7,6},{8,9},{9,8},{10,11... | collective-permute-start | bytes 393224 | tf_op jit(solution)/shard_map/ppermute | solution.py:24
  19.5 4.3 %collective-permute-start.27 = (bf16[1,2,128,256]{3,2,1,0:T(8,128)(2,1)S(1)}, bf16[1,2,128,256]{3,2,1,0:T(8,128)(2,1)S(1)}, u32[]{:S(2)}, u32[]{:S(2)}) collective-permute-start(bf16[1,2,128,256]{3,2,1,0:T(8,128)(2,1)S(1)} %collective-permute-done.23.refs_24_), channel_id=1, source_target_pairs={{0,8},{1,9},{2,10},{3,11},{4,12},{5,13},{6,14},{7,15},{8,0},{9,1},... | collective-permute-start | bytes 393224 | tf_op jit(solution)/shard_map/ppermute | solution.py:24
  19.5 6.5 %collective-permute-start.24 = (bf16[1,2,128,256]{3,2,1,0:T(8,128)(2,1)S(1)}, bf16[1,2,128,256]{3,2,1,0:T(8,128)(2,1)S(1)}, u32[]{:S(2)}, u32[]{:S(2)}) collective-permute-start(bf16[1,2,128,256]{3,2,1,0:T(8,128)(2,1)S(1)} %collective-permute-done.23.refs_24_), channel_id=1, source_target_pairs={{0,1},{1,0},{2,3},{3,2},{4,5},{5,4},{6,7},{7,6},{8,9},{9,8},{10,11... | collective-permute-start | bytes 393224 | tf_op jit(solution)/shard_map/ppermute | solution.py:24
  19.8 6.6 %collective-permute-start.29 = (bf16[1,2,128,256]{3,2,1,0:T(8,128)(2,1)S(1)}, bf16[1,2,128,256]{3,2,1,0:T(8,128)(2,1)S(1)}, u32[]{:S(2)}, u32[]{:S(2)}) collective-permute-start(bf16[1,2,128,256]{3,2,1,0:T(8,128)(2,1)S(1)} %collective-permute-done.25.refs_26_), channel_id=1, source_target_pairs={{0,8},{1,9},{2,10},{3,11},{4,12},{5,13},{6,14},{7,15},{8,0},{9,1},... | collective-permute-start | bytes 393224 | tf_op jit(solution)/shard_map/ppermute | solution.py:24
  22.1 5.3 %collective-permute-start.26 = (bf16[1,2,128,256]{3,2,1,0:T(8,128)(2,1)S(1)}, bf16[1,2,128,256]{3,2,1,0:T(8,128)(2,1)S(1)}, u32[]{:S(2)}, u32[]{:S(2)}) collective-permute-start(bf16[1,2,128,256]{3,2,1,0:T(8,128)(2,1)S(1)} %collective-permute-done.18.refs_19_), channel_id=1, source_target_pairs={{0,16},{1,17},{2,18},{3,19},{4,20},{5,21},{6,22},{7,23},{8,24},{9,... | collective-permute-start | bytes 393224 | tf_op jit(solution)/shard_map/ppermute | solution.py:24
  23.8 3.5 %collective-permute-start.22 = (bf16[1,2,128,256]{3,2,1,0:T(8,128)(2,1)S(1)}, bf16[1,2,128,256]{3,2,1,0:T(8,128)(2,1)S(1)}, u32[]{:S(2)}, u32[]{:S(2)}) collective-permute-start(bf16[1,2,128,256]{3,2,1,0:T(8,128)(2,1)S(1)} %collective-permute-done.18.refs_19_), channel_id=1, source_target_pairs={{0,8},{1,9},{2,10},{3,11},{4,12},{5,13},{6,14},{7,15},{8,0},{9,1},... | collective-permute-start | bytes 393224 | tf_op jit(solution)/shard_map/ppermute | solution.py:24
  23.8 4.7 %collective-permute-start.12 = (bf16[1,2,128,256]{3,2,1,0:T(8,128)(2,1)S(1)}, bf16[1,2,128,256]{3,2,1,0:T(8,128)(2,1)S(1)}, u32[]{:S(2)}, u32[]{:S(2)}) collective-permute-start(bf16[1,2,128,256]{3,2,1,0:T(8,128)(2,1)S(1)} %collective-permute-done.8.refs_8_), channel_id=1, source_target_pairs={{0,8},{1,9},{2,10},{3,11},{4,12},{5,13},{6,14},{7,15},{8,0},{9,1},... | collective-permute-start | bytes 393224 | tf_op jit(solution)/shard_map/ppermute | solution.py:24
  26.0 5.0 %collective-permute-start.10 = (bf16[1,2,128,256]{3,2,1,0:T(8,128)(2,1)S(1)}, bf16[1,2,128,256]{3,2,1,0:T(8,128)(2,1)S(1)}, u32[]{:S(2)}, u32[]{:S(2)}) collective-permute-start(bf16[1,2,128,256]{3,2,1,0:T(8,128)(2,1)S(1)} %collective-permute-done.8.refs_8_), channel_id=1, source_target_pairs={{0,2},{1,3},{2,0},{3,1},{4,6},{5,7},{6,4},{7,5},{8,10},{9,11},{10,... | collective-permute-start | bytes 393224 | tf_op jit(solution)/shard_map/ppermute | solution.py:24
  26.4 5.0 %collective-permute-start.3 = (bf16[1,2,128,256]{3,2,1,0:T(8,128)(2,1)S(1)}, bf16[1,2,128,256]{3,2,1,0:T(8,128)(2,1)S(1)}, u32[]{:S(2)}, u32[]{:S(2)}) collective-permute-start(bf16[1,2,128,256]{3,2,1,0:T(8,128)(2,1)S(1)} %collective-permute-done.2.refs_2_), channel_id=1, source_target_pairs={{0,1},{1,0},{2,3},{3,2},{4,5},{5,4},{6,7},{7,6},{8,9},{9,8},{10,11... | collective-permute-start | bytes 393224 | tf_op jit(solution)/shard_map/ppermute | solution.py:24
  27.3 5.2 %collective-permute-start.6 = (bf16[1,2,128,256]{3,2,1,0:T(8,128)(2,1)S(1)}, bf16[1,2,128,256]{3,2,1,0:T(8,128)(2,1)S(1)}, u32[]{:S(2)}, u32[]{:S(2)}) collective-permute-start(bf16[1,2,128,256]{3,2,1,0:T(8,128)(2,1)S(1)} %collective-permute-done.2.refs_2_), channel_id=1, source_target_pairs={{0,8},{1,9},{2,10},{3,11},{4,12},{5,13},{6,14},{7,15},{8,0},{9,1},... | collective-permute-start | bytes 393224 | tf_op jit(solution)/shard_map/ppermute | solution.py:24
  27.3 5.9 %collective-permute-start.9 = (bf16[1,2,128,256]{3,2,1,0:T(8,128)(2,1)S(1)}, bf16[1,2,128,256]{3,2,1,0:T(8,128)(2,1)S(1)}, u32[]{:S(2)}, u32[]{:S(2)}) collective-permute-start(bf16[1,2,128,256]{3,2,1,0:T(8,128)(2,1)S(1)} %collective-permute-done.1.refs_1_), channel_id=1, source_target_pairs={{0,16},{1,17},{2,18},{3,19},{4,20},{5,21},{6,22},{7,23},{8,24},{9,... | collective-permute-start | bytes 393224 | tf_op jit(solution)/shard_map/ppermute | solution.py:24
  28.5 4.7 %collective-permute-start.5 = (bf16[1,2,128,256]{3,2,1,0:T(8,128)(2,1)S(1)}, bf16[1,2,128,256]{3,2,1,0:T(8,128)(2,1)S(1)}, u32[]{:S(2)}, u32[]{:S(2)}) collective-permute-start(bf16[1,2,128,256]{3,2,1,0:T(8,128)(2,1)S(1)} %collective-permute-done.1.refs_1_), channel_id=1, source_target_pairs={{0,8},{1,9},{2,10},{3,11},{4,12},{5,13},{6,14},{7,15},{8,0},{9,1},... | collective-permute-start | bytes 393224 | tf_op jit(solution)/shard_map/ppermute | solution.py:24
  31.0 2.7 %collective-permute-start.28 = (bf16[1,2,128,256]{3,2,1,0:T(8,128)(2,1)S(1)}, bf16[1,2,128,256]{3,2,1,0:T(8,128)(2,1)S(1)}, u32[]{:S(2)}, u32[]{:S(2)}) collective-permute-start(bf16[1,2,128,256]{3,2,1,0:T(8,128)(2,1)S(1)} %collective-permute-done.24.refs_25_), channel_id=1, source_target_pairs={{0,8},{1,9},{2,10},{3,11},{4,12},{5,13},{6,14},{7,15},{8,0},{9,1},... | collective-permute-start | bytes 393224 | tf_op jit(solution)/shard_map/ppermute | solution.py:24
  31.4 5.5 %collective-permute-start.11 = (bf16[1,2,128,256]{3,2,1,0:T(8,128)(2,1)S(1)}, bf16[1,2,128,256]{3,2,1,0:T(8,128)(2,1)S(1)}, u32[]{:S(2)}, u32[]{:S(2)}) collective-permute-start(bf16[1,2,128,256]{3,2,1,0:T(8,128)(2,1)S(1)} %collective-permute-done.3.refs_3_), channel_id=1, source_target_pairs={{0,16},{1,17},{2,18},{3,19},{4,20},{5,21},{6,22},{7,23},{8,24},{9,... | collective-permute-start | bytes 393224 | tf_op jit(solution)/shard_map/ppermute | solution.py:24
  32.5 4.4 %collective-permute-start.7 = (bf16[1,2,128,256]{3,2,1,0:T(8,128)(2,1)S(1)}, bf16[1,2,128,256]{3,2,1,0:T(8,128)(2,1)S(1)}, u32[]{:S(2)}, u32[]{:S(2)}) collective-permute-start(bf16[1,2,128,256]{3,2,1,0:T(8,128)(2,1)S(1)} %collective-permute-done.3.refs_3_), channel_id=1, source_target_pairs={{0,8},{1,9},{2,10},{3,11},{4,12},{5,13},{6,14},{7,15},{8,0},{9,1},... | collective-permute-start | bytes 393224 | tf_op jit(solution)/shard_map/ppermute | solution.py:24
  33.2 3.7 %collective-permute-start.30 = (bf16[1,2,128,256]{3,2,1,0:T(8,128)(2,1)S(1)}, bf16[1,2,128,256]{3,2,1,0:T(8,128)(2,1)S(1)}, u32[]{:S(2)}, u32[]{:S(2)}) collective-permute-start(bf16[1,2,128,256]{3,2,1,0:T(8,128)(2,1)S(1)} %collective-permute-done.26.refs_27_), channel_id=1, source_target_pairs={{0,8},{1,9},{2,10},{3,11},{4,12},{5,13},{6,14},{7,15},{8,0},{9,1},... | collective-permute-start | bytes 393224 | tf_op jit(solution)/shard_map/ppermute | solution.py:24
  33.2 3.7 %collective-permute-start.14 = (bf16[1,2,128,256]{3,2,1,0:T(8,128)(2,1)S(1)}, bf16[1,2,128,256]{3,2,1,0:T(8,128)(2,1)S(1)}, u32[]{:S(2)}, u32[]{:S(2)}) collective-permute-start(bf16[1,2,128,256]{3,2,1,0:T(8,128)(2,1)S(1)} %collective-permute-done.10.refs_10_), channel_id=1, source_target_pairs={{0,8},{1,9},{2,10},{3,11},{4,12},{5,13},{6,14},{7,15},{8,0},{9,1},... | collective-permute-start | bytes 393224 | tf_op jit(solution)/shard_map/ppermute | solution.py:24
  33.8 3.2 %collective-permute-start.13 = (bf16[1,2,128,256]{3,2,1,0:T(8,128)(2,1)S(1)}, bf16[1,2,128,256]{3,2,1,0:T(8,128)(2,1)S(1)}, u32[]{:S(2)}, u32[]{:S(2)}) collective-permute-start(bf16[1,2,128,256]{3,2,1,0:T(8,128)(2,1)S(1)} %collective-permute-done.9.refs_9_), channel_id=1, source_target_pairs={{0,8},{1,9},{2,10},{3,11},{4,12},{5,13},{6,14},{7,15},{8,0},{9,1},... | collective-permute-start | bytes 393224 | tf_op jit(solution)/shard_map/ppermute | solution.py:24
  36.9 1.3 %collective-permute-start.15 = (bf16[1,2,128,256]{3,2,1,0:T(8,128)(2,1)S(1)}, bf16[1,2,128,256]{3,2,1,0:T(8,128)(2,1)S(1)}, u32[]{:S(2)}, u32[]{:S(2)}) collective-permute-start(bf16[1,2,128,256]{3,2,1,0:T(8,128)(2,1)S(1)} %collective-permute-done.11.refs_11_), channel_id=1, source_target_pairs={{0,8},{1,9},{2,10},{3,11},{4,12},{5,13},{6,14},{7,15},{8,0},{9,1},... | collective-permute-start | bytes 393224 | tf_op jit(solution)/shard_map/ppermute | solution.py:24
  38.3 0.9 copy-start
  39.2 0.7 copy-start.1
  39.9 0.7 copy-start.2
  40.5 0.7 copy-start.3
where the time goes:
time: 93.6 us; the launch traced here: 93.3 us
  blocking collectives  29.6 us (32%)
  Pallas kernels  21.6 us (23%)
  starting transfers between devices  20.6 us (22%)
  waiting for transfers between devices  17.6 us (19%)
  local copies, waits for them, and re-layouts  2.95 us (3%)
    all_to_all x1, blocking collectives, on_device(): spread = lax.all_to_all(partial, 'fit', 0, 0, tiled=True)  29.6 us
    pallas_call x1, Pallas kernels, on_device(): pl.pallas_call(functools.partial(exchange_kernel, keys, far, nq, nblk, ne...  21.6 us
    ppermute x31, starting transfers between devices, swap(): return lax.ppermute(arr, AXES, perm)  20.6 us
    ppermute x31, waiting for transfers between devices, swap(): return lax.ppermute(arr, AXES, perm)  17.6 us
    unnamed x8, local copies, waits for them, and re-layouts  2.95 us
  transfers between devices with their start and end apart: 31, of which 11 were waited for; matrix products, arithmetic and copies ran while one was open for 0% of the time, Pallas kernels for 0%

commit v1 on v0

--- a/solution.py
+++ b/solution.py
@@ -70,16 +70,39 @@
     return got, offsets[1:]
 
 
-def exchange_kernel(
-    keys, far, nq, nblk, nexch, edge, occ, nbl, match_ref, lists_ref, ex_ref, lmat_ref, *refs
+def exchange_units(order, second, unit, edge, x_ref, turned_ref, ex_ref, out_ref):
+    fit = lax.axis_index("fit")
+    half = out_ref.shape[1]
+    steps = half // unit
+    for slot, off in enumerate(order):
+        owner = lax.bitwise_xor(fit, off)
+        for step in range(steps):
+            row = owner * (2 * half) + second * half + step * unit
+            e = row // edge
+            lb, rb = ex_ref[0, 0, e], ex_ref[0, 1, e]
+            lo = pl.multiple_of(lax.rem(row, edge), unit)
+            out_ref[slot, step * unit : (step + 1) * unit, :] = jnp.dot(
+                x_ref[lb, pl.ds(lo, unit), :],
+                turned_ref[rb],
+                preferred_element_type=jnp.float32,
+            ).astype(out_ref.dtype)
+
+
+def half_kernel(
+    keys, far, orders, nq, nblk, edge, occ, nbl, match_ref, lists_ref, ex_ref, lmat_ref, *refs
 ):
     pieces = refs[: len(keys)]
-    out_ref, ops_ref, sums_ref, x_ref = refs[len(keys) :]
+    first_ref, second_ref, x_ref, turned_ref, l_ref, ops_ref, sums_ref, sems = refs[len(keys) :]
     ka, fit = lax.axis_index("ka"), lax.axis_index("fit")
     rows = pieces[0].shape[2]
     sub = min(rows, edge)
-
-    def one_q(qq, carry):
+    copies = [
+        pltpu.make_async_copy(lmat_ref.at[qq, 0, 0], l_ref.at[qq], sems.at[qq]) for qq in range(nq)
+    ]
+    for copy in copies:
+        copy.start()
+
+    for qq in range(nq):
         want = lax.bitwise_xor(match_ref[qq, ka], ka)
 
         for dka in sorted({key[1] for key in keys}):
@@ -105,43 +128,38 @@
                             ops_ref[pl.ds(low, sub), occ:] = real
 
         sums_ref[...] = jnp.zeros_like(sums_ref)
+        copies[qq].wait()
 
         def one_block(n, c):
             rb = pl.multiple_of(lists_ref[qq, 0, 0, 0, n] * edge, edge)
             cb = pl.multiple_of(lists_ref[qq, 0, 0, 1, n] * (2 * edge), 2 * edge)
             sums_ref[pl.ds(rb, edge), :] += jnp.dot(
-                lmat_ref[qq, 0, 0, n],
+                l_ref[qq, n],
                 ops_ref[pl.ds(cb, 2 * edge), :],
                 preferred_element_type=jnp.float32,
             )
             return c
 
-        lax.fori_loop(0, nblk, one_block, 0, unroll=4)
-
-        for rb in range(nbl):
-            x = sums_ref[rb * edge : (rb + 1) * edge, :].astype(jnp.bfloat16)
-            x_ref[qq, rb, :edge, :] = x
-            x_ref[qq, rb, edge:, :occ] = -x[:, occ:]
-            x_ref[qq, rb, edge:, occ:] = x[:, :occ]
-        return carry
-
-    lax.fori_loop(0, nq, one_q, 0)
-
-    def one_pair(e, c):
-        left, right = ex_ref[0, 0, e], ex_ref[0, 1, e]
-        acc = None
-        for qq in range(nq):
-            term = lax.dot_general(
-                x_ref[qq, left, :edge, :],
-                x_ref[qq, right],
-                (((1,), (1,)), ((), ())),
-                preferred_element_type=jnp.float32,
-            )
-            acc = term if acc is None else acc + term
-        out_ref[pl.ds(pl.multiple_of(e * edge, edge), edge), :] = acc.astype(out_ref.dtype)
-        return c
-
-    lax.fori_loop(0, nexch, one_pair, 0, unroll=4)
+        lax.fori_loop(0, nblk, one_block, 0, unroll=16)
+
+        def one_row(rb, c):
+            x = sums_ref[pl.ds(pl.multiple_of(rb * edge, edge), edge), :].astype(jnp.bfloat16)
+            x_ref[rb, :, qq * 2 * occ : (qq + 1) * 2 * occ] = x
+            low = jnp.concatenate([-x[:, occ:], x[:, :occ]], axis=1)
+            turned_ref[rb, qq * 2 * occ : (qq + 1) * 2 * occ, :] = jnp.concatenate([x, low], axis=0).T
+            return c
+
+        lax.fori_loop(0, nbl, one_row, 0, unroll=4)
+
+    unit = min(edge, first_ref.shape[1])
+    exchange_units(orders[0], 0, unit, edge, x_ref, turned_ref, ex_ref, first_ref)
+    exchange_units(orders[1], 1, unit, edge, x_ref, turned_ref, ex_ref, second_ref)
+
+
+def rest_kernel(orders, edge, ex_ref, x_ref, turned_ref, first_ref, second_ref):
+    unit = min(edge, first_ref.shape[1])
+    exchange_units(orders[0], 0, unit, edge, x_ref, turned_ref, ex_ref, first_ref)
+    exchange_units(orders[1], 1, unit, edge, x_ref, turned_ref, ex_ref, second_ref)
 
 
 def on_device(nka, nfit, integrals, block_lists, coeff, match, ex_blocks):
@@ -153,22 +171,74 @@
     keys = sorted(got)
     vmem = pl.BlockSpec(memory_space=pltpu.VMEM)
     smem = pl.BlockSpec(memory_space=pltpu.SMEM)
-    partial = pl.pallas_call(
-        functools.partial(exchange_kernel, keys, far, nq, nblk, nexch, edge, occ, nbl),
-        out_shape=jax.ShapeDtypeStruct((nexch * edge, 2 * edge), jnp.bfloat16),
-        in_specs=[smem, smem, smem, vmem] + [vmem] * len(keys),
-        out_specs=vmem,
+    hbm = pl.BlockSpec(memory_space=pl.ANY)
+
+    bits = bits_of(nfit)
+    ybit, wbit, rest = bits[0], bits[1], bits[2:][::-1]
+    far_offs = [0]
+    for bit in rest[::-1]:
+        far_offs = far_offs + [o ^ bit for o in far_offs]
+    keep_a = far_offs + [o ^ wbit for o in far_offs]
+    keep_b = far_offs + [o ^ ybit for o in far_offs]
+    send_a = [o ^ ybit for o in keep_a]
+    send_b = [o ^ wbit for o in keep_b]
+    half = nexch * edge // nfit // 2
+    count = len(keep_a)
+    params = pltpu.CompilerParams(vmem_limit_bytes=28 * 1024 * 1024)
+
+    def outs(dtype):
+        return [jax.ShapeDtypeStruct((count, half, 2 * edge), dtype)] * 2
+
+    xshape = (nbl, edge, nq * 2 * occ)
+    tshape = (nbl, nq * 2 * occ, 2 * edge)
+    out_a, out_b, xmat, turned = pl.pallas_call(
+        functools.partial(
+            half_kernel, keys, far, (send_a, send_b), nq, nblk, edge, occ, nbl
+        ),
+        out_shape=outs(jnp.bfloat16)
+        + [jax.ShapeDtypeStruct(xshape, jnp.bfloat16), jax.ShapeDtypeStruct(tshape, jnp.bfloat16)],
+        in_specs=[smem, smem, smem, hbm] + [vmem] * len(keys),
+        out_specs=[vmem] * 4,
         scratch_shapes=[
+            pltpu.VMEM((nq, nblk, edge, 2 * edge), jnp.bfloat16),
             pltpu.VMEM((nbl * 2 * edge, 2 * occ), jnp.bfloat16),
             pltpu.VMEM((nbl * edge, 2 * occ), jnp.float32),
-            pltpu.VMEM((nq, nbl, 2 * edge, 2 * occ), jnp.bfloat16),
+            pltpu.SemaphoreType.DMA((nq,)),
         ],
-        compiler_params=pltpu.CompilerParams(vmem_limit_bytes=48 * 1024 * 1024),
+        compiler_params=params,
     )(match, block_lists, ex_blocks, integrals, *[got[key] for key in keys])
-    spread = lax.all_to_all(partial, "fit", 0, 0, tiled=True)
+    own_a, own_b = pl.pallas_call(
+        functools.partial(rest_kernel, (keep_a, keep_b), edge),
+        out_shape=outs(jnp.float32),
+        in_specs=[smem, vmem, vmem],
+        out_specs=[vmem] * 2,
+        compiler_params=params,
+        cost_estimate=pl.CostEstimate(
+            flops=nexch * edge * edge * 2 * nq * 2 * occ, bytes_accessed=1 << 23, transcendentals=0
+        ),
+    )(ex_blocks, xmat, turned)
+
+    def swap(arr, dfit):
+        return lax.ppermute(arr, "fit", [(f, f ^ dfit) for f in range(nfit)])
+
+    def down(arr):
+        return arr.astype(jnp.bfloat16)
+
+    def up(arr):
+        return arr.astype(jnp.float32)
+
+    n = count // 2
+    got_a, got_b = swap(out_a, ybit), swap(out_b, wbit)
+    sum_a = own_a + up(got_a)
+    got_a = swap(down(sum_a[n:]), wbit)
+    sum_b = own_b + up(got_b)
+    got_b = swap(down(sum_b[n:]), ybit)
+    both = jnp.concatenate([sum_a[:n] + up(got_a), sum_b[:n] + up(got_b)], axis=1)
+    for bit in rest:
+        n = n // 2
+        both = both[:n] + up(swap(down(both[n:]), bit))
     factor = -((nq * nfit * occ) ** (-0.5))
-    parts = spread.reshape(nfit, nexch * edge // nfit, 2 * edge).astype(jnp.float32)
-    return (jnp.sum(parts, axis=0) * factor)[None]
+    return both * factor
 
 
 def solution(mesh):

time: 93.6 us -> 76.2 us (0.81)
  blocking collectives: 29.6 us -> 0 us
  waiting for transfers between devices: 17.6 us -> 30.5 us
  Pallas kernels: 21.6 us -> 13.1 us
  starting transfers between devices: 20.6 us -> 26.7 us
  local copies, waits for them, and re-layouts: 2.95 us -> 4.66 us
    all_to_all x1 -> x0, blocking collectives: 29.6 us -> none  [on_device(): spread = lax.all_to_all(partial, 'fit', 0, 0, tiled=True)]
    ppermute x0 -> x5, waiting for transfers between devices: none -> 12.9 us  [swap(): return lax.ppermute(arr, 'fit', [(f, f ^ dfit) for f in range(nfit)])]
    pallas_call x1 -> x2, Pallas kernels: 21.6 us -> 13.1 us  [the longest x1 10.2 us: on_device(): pl.pallas_call(functools.partial(half_kernel, keys, far, (send_a, send_b)...]
    ppermute x0 -> x5, starting transfers between devices: none -> 6.06 us  [swap(): return lax.ppermute(arr, 'fit', [(f, f ^ dfit) for f in range(nfit)])]
    unnamed x8 -> x12, local copies, waits for them, and re-layouts: 2.95 us -> 4.62 us
  transfers between devices with their start and end apart: 31 -> 36, of which waited for: 11 -> 15; matrix products, arithmetic and copies ran while one was open for 0% -> 0% of each run, Pallas kernels for 0% -> 4%
where the time goes in v1:
time: 76.2 us; the launch traced here: 76 us
  waiting for transfers between devices  30.5 us (40%)
  starting transfers between devices  26.7 us (35%)
  Pallas kernels  13.1 us (17%)
  local copies, waits for them, and re-layouts  4.66 us (6%)
  other arithmetic  0.92 us (1%)
    ppermute x31, starting transfers between devices, swap(): return lax.ppermute(arr, AXES, perm)  20.6 us
    ppermute x31, waiting for transfers between devices, swap(): return lax.ppermute(arr, AXES, perm)  17.6 us
    ppermute x5, waiting for transfers between devices, swap(): return lax.ppermute(arr, 'fit', [(f, f ^ dfit) for f in range(nfit)])  12.9 us
    pallas_call x1, Pallas kernels, on_device(): pl.pallas_call(functools.partial(half_kernel, keys, far, (send_a, send_b)...  10.2 us
    ppermute x5, starting transfers between devices, swap(): return lax.ppermute(arr, 'fit', [(f, f ^ dfit) for f in range(nfit)])  6.06 us
    unnamed x12, local copies, waits for them, and re-layouts  4.62 us
    pallas_call x1, Pallas kernels, on_device(): pl.pallas_call(functools.partial(rest_kernel, (keep_a, keep_b), edge), ou...  2.91 us
  transfers between devices with their start and end apart: 36, of which 15 were waited for; matrix products, arithmetic and copies ran while one was open for 0% of the time, Pallas kernels for 4%

profile of v1, /device:TPU:0, one launch (start us, length us, event | category | flops | bytes accessed | tf_op | source)
XLA Modules:
  0.0 76.0 jit_solution(14753795993683688273)
XLA Ops:
  0.0 3.0 %collective-permute-start.17 = (bf16[1,2,128,256]{3,2,1,0:T(8,128)(2,1)}, bf16[1,2,128,256]{3,2,1,0:T(8,128)(2,1)S(1)}, u32[]{:S(2)}, u32[]{:S(2)}) collective-permute-start(bf16[1,2,128,256]{3,2,1,0:T(8,128)(2,1)} %refs_16_.1), channel_id=1, source_target_pairs={{0,2},{1,3},{2,0},{3,1},{4,6},{5,7},{6,4},{7,5},{8,10},{9,11},{10,... | collective-permute-start | bytes 393224 | tf_op jit(solution)/shard_map/ppermute | solution.py:24
  3.0 1.5 %collective-permute-start.16 = (bf16[1,2,128,256]{3,2,1,0:T(8,128)(2,1)}, bf16[1,2,128,256]{3,2,1,0:T(8,128)(2,1)S(1)}, u32[]{:S(2)}, u32[]{:S(2)}) collective-permute-start(bf16[1,2,128,256]{3,2,1,0:T(8,128)(2,1)} %refs_16_.1), channel_id=1, source_target_pairs={{0,1},{1,0},{2,3},{3,2},{4,5},{5,4},{6,7},{7,6},{8,9},{9,8},{10,11... | collective-permute-start | bytes 393224 | tf_op jit(solution)/shard_map/ppermute | solution.py:24
  4.5 2.6 %collective-permute-start = (bf16[1,2,128,256]{3,2,1,0:T(8,128)(2,1)}, bf16[1,2,128,256]{3,2,1,0:T(8,128)(2,1)S(1)}, u32[]{:S(2)}, u32[]{:S(2)}) collective-permute-start(bf16[1,2,128,256]{3,2,1,0:T(8,128)(2,1)} %refs_16_.1), channel_id=1, source_target_pairs={{0,4},{1,5},{2,6},{3,7},{4,0},{5,1},{6,2},{7,3},{8,12},{9,13},{10,... | collective-permute-start | bytes 393224 | tf_op jit(solution)/shard_map/ppermute | solution.py:24
  7.1 1.5 %collective-permute-start.23 = (bf16[1,2,128,256]{3,2,1,0:T(8,128)(2,1)}, bf16[1,2,128,256]{3,2,1,0:T(8,128)(2,1)S(1)}, u32[]{:S(2)}, u32[]{:S(2)}) collective-permute-start(bf16[1,2,128,256]{3,2,1,0:T(8,128)(2,1)} %refs_16_.1), channel_id=1, source_target_pairs={{0,16},{1,17},{2,18},{3,19},{4,20},{5,21},{6,22},{7,23},{8,24},{9,... | collective-permute-start | bytes 393224 | tf_op jit(solution)/shard_map/ppermute | solution.py:24
  8.6 0.5 collective-permute-start.25
  9.2 0.5 collective-permute-start.20
  9.7 4.4 %collective-permute-done.refs_0_ = bf16[1,2,128,256]{3,2,1,0:T(8,128)(2,1)S(1)} collective-permute-done((bf16[1,2,128,256]{3,2,1,0:T(8,128)(2,1)}, bf16[1,2,128,256]{3,2,1,0:T(8,128)(2,1)S(1)}, u32[]{:S(2)}, u32[]{:S(2)}) %collective-permute-start) | collective-permute-done | bytes 131104 | tf_op jit(solution)/shard_map/ppermute | solution.py:24
  14.1 1.5 %collective-permute-start.8 = (bf16[1,2,128,256]{3,2,1,0:T(8,128)(2,1)S(1)}, bf16[1,2,128,256]{3,2,1,0:T(8,128)(2,1)S(1)}, u32[]{:S(2)}, u32[]{:S(2)}) collective-permute-start(bf16[1,2,128,256]{3,2,1,0:T(8,128)(2,1)S(1)} %collective-permute-done.refs_0_), channel_id=1, source_target_pairs={{0,16},{1,17},{2,18},{3,19},{4,20},{5,21},{6,22},{7,23},{8,24},{9,... | collective-permute-start | bytes 393224 | tf_op jit(solution)/shard_map/ppermute | solution.py:24
  15.6 2.1 %collective-permute-start.2 = (bf16[1,2,128,256]{3,2,1,0:T(8,128)(2,1)S(1)}, bf16[1,2,128,256]{3,2,1,0:T(8,128)(2,1)S(1)}, u32[]{:S(2)}, u32[]{:S(2)}) collective-permute-start(bf16[1,2,128,256]{3,2,1,0:T(8,128)(2,1)S(1)} %collective-permute-done.refs_0_), channel_id=1, source_target_pairs={{0,2},{1,3},{2,0},{3,1},{4,6},{5,7},{6,4},{7,5},{8,10},{9,11},{10,... | collective-permute-start | bytes 393224 | tf_op jit(solution)/shard_map/ppermute | solution.py:24
  17.7 0.6 collective-permute-start.1
  18.2 1.3 %collective-permute-done.18.refs_19_ = bf16[1,2,128,256]{3,2,1,0:T(8,128)(2,1)S(1)} collective-permute-done((bf16[1,2,128,256]{3,2,1,0:T(8,128)(2,1)S(1)}, bf16[1,2,128,256]{3,2,1,0:T(8,128)(2,1)S(1)}, u32[]{:S(2)}, u32[]{:S(2)}) %collective-permute-start.18) | collective-permute-done | bytes 131104 | tf_op jit(solution)/shard_map/ppermute | solution.py:24
  19.5 0.3 collective-permute-start.24
  19.8 0.3 collective-permute-start.29
  20.1 2.0 %collective-permute-done.2.refs_2_ = bf16[1,2,128,256]{3,2,1,0:T(8,128)(2,1)S(1)} collective-permute-done((bf16[1,2,128,256]{3,2,1,0:T(8,128)(2,1)S(1)}, bf16[1,2,128,256]{3,2,1,0:T(8,128)(2,1)S(1)}, u32[]{:S(2)}, u32[]{:S(2)}) %collective-permute-start.2) | collective-permute-done | bytes 131104 | tf_op jit(solution)/shard_map/ppermute | solution.py:24
  22.1 1.5 %collective-permute-start.26 = (bf16[1,2,128,256]{3,2,1,0:T(8,128)(2,1)S(1)}, bf16[1,2,128,256]{3,2,1,0:T(8,128)(2,1)S(1)}, u32[]{:S(2)}, u32[]{:S(2)}) collective-permute-start(bf16[1,2,128,256]{3,2,1,0:T(8,128)(2,1)S(1)} %collective-permute-done.18.refs_19_), channel_id=1, source_target_pairs={{0,16},{1,17},{2,18},{3,19},{4,20},{5,21},{6,22},{7,23},{8,24},{9,... | collective-permute-start | bytes 393224 | tf_op jit(solution)/shard_map/ppermute | solution.py:24
  23.6 0.2 collective-permute-done.1.refs_1_
  23.8 0.5 collective-permute-start.12
  24.3 1.7 %collective-permute-done.24.refs_25_ = bf16[1,2,128,256]{3,2,1,0:T(8,128)(2,1)S(1)} collective-permute-done((bf16[1,2,128,256]{3,2,1,0:T(8,128)(2,1)S(1)}, bf16[1,2,128,256]{3,2,1,0:T(8,128)(2,1)S(1)}, u32[]{:S(2)}, u32[]{:S(2)}) %collective-permute-start.24) | collective-permute-done | bytes 131104 | tf_op jit(solution)/shard_map/ppermute | solution.py:24
  26.0 0.4 collective-permute-start.10
  26.4 0.6 collective-permute-start.3
  27.0 0.4 collective-permute-done.26.refs_27_
  27.3 1.2 %collective-permute-start.9 = (bf16[1,2,128,256]{3,2,1,0:T(8,128)(2,1)S(1)}, bf16[1,2,128,256]{3,2,1,0:T(8,128)(2,1)S(1)}, u32[]{:S(2)}, u32[]{:S(2)}) collective-permute-start(bf16[1,2,128,256]{3,2,1,0:T(8,128)(2,1)S(1)} %collective-permute-done.1.refs_1_), channel_id=1, source_target_pairs={{0,16},{1,17},{2,18},{3,19},{4,20},{5,21},{6,22},{7,23},{8,24},{9,... | collective-permute-start | bytes 393224 | tf_op jit(solution)/shard_map/ppermute | solution.py:24
  28.5 0.2 collective-permute-start.5
  28.8 2.2 %collective-permute-done.10.refs_10_ = bf16[1,2,128,256]{3,2,1,0:T(8,128)(2,1)S(1)} collective-permute-done((bf16[1,2,128,256]{3,2,1,0:T(8,128)(2,1)S(1)}, bf16[1,2,128,256]{3,2,1,0:T(8,128)(2,1)S(1)}, u32[]{:S(2)}, u32[]{:S(2)}) %collective-permute-start.10) | collective-permute-done | bytes 131104 | tf_op jit(solution)/shard_map/ppermute | solution.py:24
  31.0 0.4 collective-permute-done.3.refs_3_
  31.4 1.1 %collective-permute-start.11 = (bf16[1,2,128,256]{3,2,1,0:T(8,128)(2,1)S(1)}, bf16[1,2,128,256]{3,2,1,0:T(8,128)(2,1)S(1)}, u32[]{:S(2)}, u32[]{:S(2)}) collective-permute-start(bf16[1,2,128,256]{3,2,1,0:T(8,128)(2,1)S(1)} %collective-permute-done.3.refs_3_), channel_id=1, source_target_pairs={{0,16},{1,17},{2,18},{3,19},{4,20},{5,21},{6,22},{7,23},{8,24},{9,... | collective-permute-start | bytes 393224 | tf_op jit(solution)/shard_map/ppermute | solution.py:24
  32.5 0.2 collective-permute-start.7
  32.7 0.6 collective-permute-done.9.refs_9_
  33.2 0.5 collective-permute-start.14
  33.8 3.1 %collective-permute-done.11.refs_11_ = bf16[1,2,128,256]{3,2,1,0:T(8,128)(2,1)S(1)} collective-permute-done((bf16[1,2,128,256]{3,2,1,0:T(8,128)(2,1)S(1)}, bf16[1,2,128,256]{3,2,1,0:T(8,128)(2,1)S(1)}, u32[]{:S(2)}, u32[]{:S(2)}) %collective-permute-start.11) | collective-permute-done | bytes 131104 | tf_op jit(solution)/shard_map/ppermute | solution.py:24
  37.0 1.3 %collective-permute-done.15.refs_15_ = bf16[1,2,128,256]{3,2,1,0:T(8,128)(2,1)S(1)} collective-permute-done((bf16[1,2,128,256]{3,2,1,0:T(8,128)(2,1)S(1)}, bf16[1,2,128,256]{3,2,1,0:T(8,128)(2,1)S(1)}, u32[]{:S(2)}, u32[]{:S(2)}) %collective-permute-start.15) | collective-permute-done | bytes 131104 | tf_op jit(solution)/shard_map/ppermute | solution.py:24
  38.3 1.7 %copy-done = bf16[3,1,1,48,64,128]{5,4,3,2,1,0:T(8,128)(2,1)S(1)} copy-done((bf16[3,1,1,48,64,128]{5,4,3,2,1,0:T(8,128)(2,1)S(1)}, bf16[3,1,1,48,64,128]{5,4,3,2,1,0:T(8,128)(2,1)}, u32[]{:S(2)}) %copy-start) | copy-done | bytes 2359320
  39.9 0.9 %copy-done.1 = bf16[1,2,128,256]{3,2,1,0:T(8,128)(2,1)S(1)} copy-done((bf16[1,2,128,256]{3,2,1,0:T(8,128)(2,1)S(1)}, bf16[1,2,128,256]{3,2,1,0:T(8,128)(2,1)}, u32[]{:S(2)}) %copy-start.1) | copy-done | bytes 131096
  40.8 0.7 copy-done.2
  41.5 0.7 copy-done.4
  42.2 0.7 copy-done.5
  42.9 10.2 %shard_map.55 = (bf16[4,256,128]{2,1,0:T(8,128)(2,1)S(1)}, bf16[4,256,128]{2,1,0:T(8,128)(2,1)S(1)}, bf16[16,64,1536]{2,1,0:T(8,128)(2,1)S(1)}, bf16[16,1536,128]{2,1,0:T(8,128)(2,1)S(1)}) custom-call(s32[3,4]{1,0:T(4,128)S(1)} %copy-done.5, s32[3,1,1,2,48]{4,3,2,1,0:T(2,128)S(1)} %copy-done.4, s32[1,2,64]{2,1,0:T(2,128)S(1)} %copy-done.2, ...), custom_call_target="tpu_custom_call" | custom-call | tf_op jit(solution)/shard_map/pallas_call | solution.py:194
  53.1 0.6 collective-permute-start.31
  53.7 1.4 %collective-permute-start.33 = (bf16[4,256,128]{2,1,0:T(8,128)(2,1)S(1)}, bf16[4,256,128]{2,1,0:T(8,128)(2,1)S(1)}, u32[]{:S(2)}, u32[]{:S(2)}) collective-permute-start(bf16[4,256,128]{2,1,0:T(8,128)(2,1)S(1)} %get-tuple-element.16), channel_id=1, source_target_pairs={{0,2},{1,3},{2,0},{3,1},{4,6},{5,7},{6,4},{7,5},{8,10},{9,11},{10,... | collective-permute-start | bytes 786440 | tf_op jit(solution)/shard_map/ppermute | solution.py:222
  55.1 2.9 %shard_map.56 = (f32[4,256,128]{2,1,0:T(8,128)S(1)}, f32[4,256,128]{2,1,0:T(8,128)S(1)}) custom-call(s32[1,2,64]{2,1,0:T(2,128)S(1)} %copy-done.3, bf16[16,64,1536]{2,1,0:T(8,128)(2,1)S(1)} %get-tuple-element.11.x_ref, bf16[16,1536,128]{2,1,0:T(8,128)(2,1)S(1)} %get-tuple-element.12.turned_ref), custom_call_target="tpu_custom_call" | custom-call | flops 805306368 | bytes 8388608 | tf_op jit(solution)/shard_map/pallas_call | solution.py:210
  58.0 3.5 %collective-permute-done.31 = bf16[4,256,128]{2,1,0:T(8,128)(2,1)S(1)} collective-permute-done((bf16[4,256,128]{2,1,0:T(8,128)(2,1)S(1)}, bf16[4,256,128]{2,1,0:T(8,128)(2,1)S(1)}, u32[]{:S(2)}, u32[]{:S(2)}) %collective-permute-start.31) | collective-permute-done | bytes 262176 | tf_op jit(solution)/shard_map/ppermute | solution.py:222
  61.6 1.1 %collective-permute-start.32 = (bf16[2,256,128]{2,1,0:T(8,128)(2,1)S(1)}, bf16[2,256,128]{2,1,0:T(8,128)(2,1)S(1)}, u32[]{:S(2)}, u32[]{:S(2)}) collective-permute-start(bf16[2,256,128]{2,1,0:T(8,128)(2,1)S(1)} %slice.48), channel_id=1, source_target_pairs={{0,2},{1,3},{2,0},{3,1},{4,6},{5,7},{6,4},{7,5},{8,10},{9,11},{10,... | collective-permute-start | bytes 393224 | tf_op jit(solution)/shard_map/ppermute | solution.py:222
  62.8 0.9 %collective-permute-start.34 = (bf16[2,256,128]{2,1,0:T(8,128)(2,1)S(1)}, bf16[2,256,128]{2,1,0:T(8,128)(2,1)S(1)}, u32[]{:S(2)}, u32[]{:S(2)}) collective-permute-start(bf16[2,256,128]{2,1,0:T(8,128)(2,1)S(1)} %slice.47), channel_id=1, source_target_pairs={{0,1},{1,0},{2,3},{3,2},{4,5},{5,4},{6,7},{7,6},{8,9},{9,8},{10,11... | collective-permute-start | bytes 393224 | tf_op jit(solution)/shard_map/ppermute | solution.py:222
  63.7 2.9 %collective-permute-done.32 = bf16[2,256,128]{2,1,0:T(8,128)(2,1)S(1)} collective-permute-done((bf16[2,256,128]{2,1,0:T(8,128)(2,1)S(1)}, bf16[2,256,128]{2,1,0:T(8,128)(2,1)S(1)}, u32[]{:S(2)}, u32[]{:S(2)}) %collective-permute-start.32) | collective-permute-done | bytes 131104 | tf_op jit(solution)/shard_map/ppermute | solution.py:222
  66.7 1.2 %collective-permute-done.34 = bf16[2,256,128]{2,1,0:T(8,128)(2,1)S(1)} collective-permute-done((bf16[2,256,128]{2,1,0:T(8,128)(2,1)S(1)}, bf16[2,256,128]{2,1,0:T(8,128)(2,1)S(1)}, u32[]{:S(2)}, u32[]{:S(2)}) %collective-permute-start.34) | collective-permute-done | bytes 131104 | tf_op jit(solution)/shard_map/ppermute | solution.py:222
  67.9 2.1 %collective-permute-start.35 = (bf16[1,512,128]{2,1,0:T(8,128)(2,1)S(1)}, bf16[1,512,128]{2,1,0:T(8,128)(2,1)S(1)}, u32[]{:S(2)}, u32[]{:S(2)}) collective-permute-start(bf16[1,512,128]{2,1,0:T(8,128)(2,1)S(1)} %fusion.3), channel_id=1, source_target_pairs={{0,4},{1,5},{2,6},{3,7},{4,0},{5,1},{6,2},{7,3},{8,12},{9,13},{10,... | collective-permute-start | bytes 393224 | tf_op jit(solution)/shard_map/ppermute | solution.py:222
  70.0 5.3 %collective-permute-done.35 = bf16[1,512,128]{2,1,0:T(8,128)(2,1)S(1)} collective-permute-done((bf16[1,512,128]{2,1,0:T(8,128)(2,1)S(1)}, bf16[1,512,128]{2,1,0:T(8,128)(2,1)S(1)}, u32[]{:S(2)}, u32[]{:S(2)}) %collective-permute-start.35) | collective-permute-done | bytes 131104 | tf_op jit(solution)/shard_map/ppermute | solution.py:222
  75.2 0.7 fusion.2
  (46 shorter events, 0.4 us)
Async XLA Ops:
  0.0 8.6 %collective-permute-start.17 = (bf16[1,2,128,256]{3,2,1,0:T(8,128)(2,1)}, bf16[1,2,128,256]{3,2,1,0:T(8,128)(2,1)S(1)}, u32[]{:S(2)}, u32[]{:S(2)}) collective-permute-start(bf16[1,2,128,256]{3,2,1,0:T(8,128)(2,1)} %refs_16_.1), channel_id=1, source_target_pairs={{0,2},{1,3},{2,0},{3,1},{4,6},{5,7},{6,4},{7,5},{8,10},{9,11},{10,... | collective-permute-start | bytes 393224 | tf_op jit(solution)/shard_map/ppermute | solution.py:24
  3.0 6.1 %collective-permute-start.19 = (bf16[1,2,128,256]{3,2,1,0:T(8,128)(2,1)}, bf16[1,2,128,256]{3,2,1,0:T(8,128)(2,1)S(1)}, u32[]{:S(2)}, u32[]{:S(2)}) collective-permute-start(bf16[1,2,128,256]{3,2,1,0:T(8,128)(2,1)} %refs_16_.1), channel_id=1, source_target_pairs={{0,8},{1,9},{2,10},{3,11},{4,12},{5,13},{6,14},{7,15},{8,0},{9,1},... | collective-permute-start | bytes 393224 | tf_op jit(solution)/shard_map/ppermute | solution.py:24
  3.0 6.1 %collective-permute-start.16 = (bf16[1,2,128,256]{3,2,1,0:T(8,128)(2,1)}, bf16[1,2,128,256]{3,2,1,0:T(8,128)(2,1)S(1)}, u32[]{:S(2)}, u32[]{:S(2)}) collective-permute-start(bf16[1,2,128,256]{3,2,1,0:T(8,128)(2,1)} %refs_16_.1), channel_id=1, source_target_pairs={{0,1},{1,0},{2,3},{3,2},{4,5},{5,4},{6,7},{7,6},{8,9},{9,8},{10,11... | collective-permute-start | bytes 393224 | tf_op jit(solution)/shard_map/ppermute | solution.py:24
  4.5 9.5 %collective-permute-start = (bf16[1,2,128,256]{3,2,1,0:T(8,128)(2,1)}, bf16[1,2,128,256]{3,2,1,0:T(8,128)(2,1)S(1)}, u32[]{:S(2)}, u32[]{:S(2)}) collective-permute-start(bf16[1,2,128,256]{3,2,1,0:T(8,128)(2,1)} %refs_16_.1), channel_id=1, source_target_pairs={{0,4},{1,5},{2,6},{3,7},{4,0},{5,1},{6,2},{7,3},{8,12},{9,13},{10,... | collective-permute-start | bytes 393224 | tf_op jit(solution)/shard_map/ppermute | solution.py:24
  7.1 6.9 %collective-permute-start.23 = (bf16[1,2,128,256]{3,2,1,0:T(8,128)(2,1)}, bf16[1,2,128,256]{3,2,1,0:T(8,128)(2,1)S(1)}, u32[]{:S(2)}, u32[]{:S(2)}) collective-permute-start(bf16[1,2,128,256]{3,2,1,0:T(8,128)(2,1)} %refs_16_.1), channel_id=1, source_target_pairs={{0,16},{1,17},{2,18},{3,19},{4,20},{5,21},{6,22},{7,23},{8,24},{9,... | collective-permute-start | bytes 393224 | tf_op jit(solution)/shard_map/ppermute | solution.py:24
  8.6 6.9 %collective-permute-start.25 = (bf16[1,2,128,256]{3,2,1,0:T(8,128)(2,1)S(1)}, bf16[1,2,128,256]{3,2,1,0:T(8,128)(2,1)S(1)}, u32[]{:S(2)}, u32[]{:S(2)}) collective-permute-start(bf16[1,2,128,256]{3,2,1,0:T(8,128)(2,1)S(1)} %collective-permute-done.17.refs_18_), channel_id=1, source_target_pairs={{0,16},{1,17},{2,18},{3,19},{4,20},{5,21},{6,22},{7,23},{8,24},{9,... | collective-permute-start | bytes 393224 | tf_op jit(solution)/shard_map/ppermute | solution.py:24
  9.2 6.4 %collective-permute-start.21 = (bf16[1,2,128,256]{3,2,1,0:T(8,128)(2,1)S(1)}, bf16[1,2,128,256]{3,2,1,0:T(8,128)(2,1)S(1)}, u32[]{:S(2)}, u32[]{:S(2)}) collective-permute-start(bf16[1,2,128,256]{3,2,1,0:T(8,128)(2,1)S(1)} %collective-permute-done.17.refs_18_), channel_id=1, source_target_pairs={{0,8},{1,9},{2,10},{3,11},{4,12},{5,13},{6,14},{7,15},{8,0},{9,1},... | collective-permute-start | bytes 393224 | tf_op jit(solution)/shard_map/ppermute | solution.py:24
  9.2 8.5 %collective-permute-start.20 = (bf16[1,2,128,256]{3,2,1,0:T(8,128)(2,1)S(1)}, bf16[1,2,128,256]{3,2,1,0:T(8,128)(2,1)S(1)}, u32[]{:S(2)}, u32[]{:S(2)}) collective-permute-start(bf16[1,2,128,256]{3,2,1,0:T(8,128)(2,1)S(1)} %collective-permute-done.16.refs_17_), channel_id=1, source_target_pairs={{0,8},{1,9},{2,10},{3,11},{4,12},{5,13},{6,14},{7,15},{8,0},{9,1},... | collective-permute-start | bytes 393224 | tf_op jit(solution)/shard_map/ppermute | solution.py:24
  14.1 5.4 %collective-permute-start.18 = (bf16[1,2,128,256]{3,2,1,0:T(8,128)(2,1)S(1)}, bf16[1,2,128,256]{3,2,1,0:T(8,128)(2,1)S(1)}, u32[]{:S(2)}, u32[]{:S(2)}) collective-permute-start(bf16[1,2,128,256]{3,2,1,0:T(8,128)(2,1)S(1)} %collective-permute-done.16.refs_17_), channel_id=1, source_target_pairs={{0,2},{1,3},{2,0},{3,1},{4,6},{5,7},{6,4},{7,5},{8,10},{9,11},{10,... | collective-permute-start | bytes 393224 | tf_op jit(solution)/shard_map/ppermute | solution.py:24
  14.1 5.4 %collective-permute-start.8 = (bf16[1,2,128,256]{3,2,1,0:T(8,128)(2,1)S(1)}, bf16[1,2,128,256]{3,2,1,0:T(8,128)(2,1)S(1)}, u32[]{:S(2)}, u32[]{:S(2)}) collective-permute-start(bf16[1,2,128,256]{3,2,1,0:T(8,128)(2,1)S(1)} %collective-permute-done.refs_0_), channel_id=1, source_target_pairs={{0,16},{1,17},{2,18},{3,19},{4,20},{5,21},{6,22},{7,23},{8,24},{9,... | collective-permute-start | bytes 393224 | tf_op jit(solution)/shard_map/ppermute | solution.py:24
  15.6 4.2 %collective-permute-start.4 = (bf16[1,2,128,256]{3,2,1,0:T(8,128)(2,1)S(1)}, bf16[1,2,128,256]{3,2,1,0:T(8,128)(2,1)S(1)}, u32[]{:S(2)}, u32[]{:S(2)}) collective-permute-start(bf16[1,2,128,256]{3,2,1,0:T(8,128)(2,1)S(1)} %collective-permute-done.refs_0_), channel_id=1, source_target_pairs={{0,8},{1,9},{2,10},{3,11},{4,12},{5,13},{6,14},{7,15},{8,0},{9,1},... | collective-permute-start | bytes 393224 | tf_op jit(solution)/shard_map/ppermute | solution.py:24
  15.6 6.5 %collective-permute-start.2 = (bf16[1,2,128,256]{3,2,1,0:T(8,128)(2,1)S(1)}, bf16[1,2,128,256]{3,2,1,0:T(8,128)(2,1)S(1)}, u32[]{:S(2)}, u32[]{:S(2)}) collective-permute-start(bf16[1,2,128,256]{3,2,1,0:T(8,128)(2,1)S(1)} %collective-permute-done.refs_0_), channel_id=1, source_target_pairs={{0,2},{1,3},{2,0},{3,1},{4,6},{5,7},{6,4},{7,5},{8,10},{9,11},{10,... | collective-permute-start | bytes 393224 | tf_op jit(solution)/shard_map/ppermute | solution.py:24
  17.7 6.1 %collective-permute-start.1 = (bf16[1,2,128,256]{3,2,1,0:T(8,128)(2,1)S(1)}, bf16[1,2,128,256]{3,2,1,0:T(8,128)(2,1)S(1)}, u32[]{:S(2)}, u32[]{:S(2)}) collective-permute-start(bf16[1,2,128,256]{3,2,1,0:T(8,128)(2,1)S(1)} %collective-permute-done.refs_0_), channel_id=1, source_target_pairs={{0,1},{1,0},{2,3},{3,2},{4,5},{5,4},{6,7},{7,6},{8,9},{9,8},{10,11... | collective-permute-start | bytes 393224 | tf_op jit(solution)/shard_map/ppermute | solution.py:24
  19.5 4.3 %collective-permute-start.27 = (bf16[1,2,128,256]{3,2,1,0:T(8,128)(2,1)S(1)}, bf16[1,2,128,256]{3,2,1,0:T(8,128)(2,1)S(1)}, u32[]{:S(2)}, u32[]{:S(2)}) collective-permute-start(bf16[1,2,128,256]{3,2,1,0:T(8,128)(2,1)S(1)} %collective-permute-done.23.refs_24_), channel_id=1, source_target_pairs={{0,8},{1,9},{2,10},{3,11},{4,12},{5,13},{6,14},{7,15},{8,0},{9,1},... | collective-permute-start | bytes 393224 | tf_op jit(solution)/shard_map/ppermute | solution.py:24
  19.5 6.5 %collective-permute-start.24 = (bf16[1,2,128,256]{3,2,1,0:T(8,128)(2,1)S(1)}, bf16[1,2,128,256]{3,2,1,0:T(8,128)(2,1)S(1)}, u32[]{:S(2)}, u32[]{:S(2)}) collective-permute-start(bf16[1,2,128,256]{3,2,1,0:T(8,128)(2,1)S(1)} %collective-permute-done.23.refs_24_), channel_id=1, source_target_pairs={{0,1},{1,0},{2,3},{3,2},{4,5},{5,4},{6,7},{7,6},{8,9},{9,8},{10,11... | collective-permute-start | bytes 393224 | tf_op jit(solution)/shard_map/ppermute | solution.py:24
  19.8 6.6 %collective-permute-start.29 = (bf16[1,2,128,256]{3,2,1,0:T(8,128)(2,1)S(1)}, bf16[1,2,128,256]{3,2,1,0:T(8,128)(2,1)S(1)}, u32[]{:S(2)}, u32[]{:S(2)}) collective-permute-start(bf16[1,2,128,256]{3,2,1,0:T(8,128)(2,1)S(1)} %collective-permute-done.25.refs_26_), channel_id=1, source_target_pairs={{0,8},{1,9},{2,10},{3,11},{4,12},{5,13},{6,14},{7,15},{8,0},{9,1},... | collective-permute-start | bytes 393224 | tf_op jit(solution)/shard_map/ppermute | solution.py:24
  22.1 5.3 %collective-permute-start.26 = (bf16[1,2,128,256]{3,2,1,0:T(8,128)(2,1)S(1)}, bf16[1,2,128,256]{3,2,1,0:T(8,128)(2,1)S(1)}, u32[]{:S(2)}, u32[]{:S(2)}) collective-permute-start(bf16[1,2,128,256]{3,2,1,0:T(8,128)(2,1)S(1)} %collective-permute-done.18.refs_19_), channel_id=1, source_target_pairs={{0,16},{1,17},{2,18},{3,19},{4,20},{5,21},{6,22},{7,23},{8,24},{9,... | collective-permute-start | bytes 393224 | tf_op jit(solution)/shard_map/ppermute | solution.py:24
  23.8 3.5 %collective-permute-start.22 = (bf16[1,2,128,256]{3,2,1,0:T(8,128)(2,1)S(1)}, bf16[1,2,128,256]{3,2,1,0:T(8,128)(2,1)S(1)}, u32[]{:S(2)}, u32[]{:S(2)}) collective-permute-start(bf16[1,2,128,256]{3,2,1,0:T(8,128)(2,1)S(1)} %collective-permute-done.18.refs_19_), channel_id=1, source_target_pairs={{0,8},{1,9},{2,10},{3,11},{4,12},{5,13},{6,14},{7,15},{8,0},{9,1},... | collective-permute-start | bytes 393224 | tf_op jit(solution)/shard_map/ppermute | solution.py:24
  23.8 4.7 %collective-permute-start.12 = (bf16[1,2,128,256]{3,2,1,0:T(8,128)(2,1)S(1)}, bf16[1,2,128,256]{3,2,1,0:T(8,128)(2,1)S(1)}, u32[]{:S(2)}, u32[]{:S(2)}) collective-permute-start(bf16[1,2,128,256]{3,2,1,0:T(8,128)(2,1)S(1)} %collective-permute-done.8.refs_8_), channel_id=1, source_target_pairs={{0,8},{1,9},{2,10},{3,11},{4,12},{5,13},{6,14},{7,15},{8,0},{9,1},... | collective-permute-start | bytes 393224 | tf_op jit(solution)/shard_map/ppermute | solution.py:24
  26.0 5.0 %collective-permute-start.10 = (bf16[1,2,128,256]{3,2,1,0:T(8,128)(2,1)S(1)}, bf16[1,2,128,256]{3,2,1,0:T(8,128)(2,1)S(1)}, u32[]{:S(2)}, u32[]{:S(2)}) collective-permute-start(bf16[1,2,128,256]{3,2,1,0:T(8,128)(2,1)S(1)} %collective-permute-done.8.refs_8_), channel_id=1, source_target_pairs={{0,2},{1,3},{2,0},{3,1},{4,6},{5,7},{6,4},{7,5},{8,10},{9,11},{10,... | collective-permute-start | bytes 393224 | tf_op jit(solution)/shard_map/ppermute | solution.py:24
  26.4 5.0 %collective-permute-start.3 = (bf16[1,2,128,256]{3,2,1,0:T(8,128)(2,1)S(1)}, bf16[1,2,128,256]{3,2,1,0:T(8,128)(2,1)S(1)}, u32[]{:S(2)}, u32[]{:S(2)}) collective-permute-start(bf16[1,2,128,256]{3,2,1,0:T(8,128)(2,1)S(1)} %collective-permute-done.2.refs_2_), channel_id=1, source_target_pairs={{0,1},{1,0},{2,3},{3,2},{4,5},{5,4},{6,7},{7,6},{8,9},{9,8},{10,11... | collective-permute-start | bytes 393224 | tf_op jit(solution)/shard_map/ppermute | solution.py:24
  27.3 5.2 %collective-permute-start.6 = (bf16[1,2,128,256]{3,2,1,0:T(8,128)(2,1)S(1)}, bf16[1,2,128,256]{3,2,1,0:T(8,128)(2,1)S(1)}, u32[]{:S(2)}, u32[]{:S(2)}) collective-permute-start(bf16[1,2,128,256]{3,2,1,0:T(8,128)(2,1)S(1)} %collective-permute-done.2.refs_2_), channel_id=1, source_target_pairs={{0,8},{1,9},{2,10},{3,11},{4,12},{5,13},{6,14},{7,15},{8,0},{9,1},... | collective-permute-start | bytes 393224 | tf_op jit(solution)/shard_map/ppermute | solution.py:24
  27.3 5.9 %collective-permute-start.9 = (bf16[1,2,128,256]{3,2,1,0:T(8,128)(2,1)S(1)}, bf16[1,2,128,256]{3,2,1,0:T(8,128)(2,1)S(1)}, u32[]{:S(2)}, u32[]{:S(2)}) collective-permute-start(bf16[1,2,128,256]{3,2,1,0:T(8,128)(2,1)S(1)} %collective-permute-done.1.refs_1_), channel_id=1, source_target_pairs={{0,16},{1,17},{2,18},{3,19},{4,20},{5,21},{6,22},{7,23},{8,24},{9,... | collective-permute-start | bytes 393224 | tf_op jit(solution)/shard_map/ppermute | solution.py:24
  28.5 4.7 %collective-permute-start.5 = (bf16[1,2,128,256]{3,2,1,0:T(8,128)(2,1)S(1)}, bf16[1,2,128,256]{3,2,1,0:T(8,128)(2,1)S(1)}, u32[]{:S(2)}, u32[]{:S(2)}) collective-permute-start(bf16[1,2,128,256]{3,2,1,0:T(8,128)(2,1)S(1)} %collective-permute-done.1.refs_1_), channel_id=1, source_target_pairs={{0,8},{1,9},{2,10},{3,11},{4,12},{5,13},{6,14},{7,15},{8,0},{9,1},... | collective-permute-start | bytes 393224 | tf_op jit(solution)/shard_map/ppermute | solution.py:24
  31.0 2.7 %collective-permute-start.28 = (bf16[1,2,128,256]{3,2,1,0:T(8,128)(2,1)S(1)}, bf16[1,2,128,256]{3,2,1,0:T(8,128)(2,1)S(1)}, u32[]{:S(2)}, u32[]{:S(2)}) collective-permute-start(bf16[1,2,128,256]{3,2,1,0:T(8,128)(2,1)S(1)} %collective-permute-done.24.refs_25_), channel_id=1, source_target_pairs={{0,8},{1,9},{2,10},{3,11},{4,12},{5,13},{6,14},{7,15},{8,0},{9,1},... | collective-permute-start | bytes 393224 | tf_op jit(solution)/shard_map/ppermute | solution.py:24
  31.4 5.5 %collective-permute-start.11 = (bf16[1,2,128,256]{3,2,1,0:T(8,128)(2,1)S(1)}, bf16[1,2,128,256]{3,2,1,0:T(8,128)(2,1)S(1)}, u32[]{:S(2)}, u32[]{:S(2)}) collective-permute-start(bf16[1,2,128,256]{3,2,1,0:T(8,128)(2,1)S(1)} %collective-permute-done.3.refs_3_), channel_id=1, source_target_pairs={{0,16},{1,17},{2,18},{3,19},{4,20},{5,21},{6,22},{7,23},{8,24},{9,... | collective-permute-start | bytes 393224 | tf_op jit(solution)/shard_map/ppermute | solution.py:24
  32.5 4.4 %collective-permute-start.7 = (bf16[1,2,128,256]{3,2,1,0:T(8,128)(2,1)S(1)}, bf16[1,2,128,256]{3,2,1,0:T(8,128)(2,1)S(1)}, u32[]{:S(2)}, u32[]{:S(2)}) collective-permute-start(bf16[1,2,128,256]{3,2,1,0:T(8,128)(2,1)S(1)} %collective-permute-done.3.refs_3_), channel_id=1, source_target_pairs={{0,8},{1,9},{2,10},{3,11},{4,12},{5,13},{6,14},{7,15},{8,0},{9,1},... | collective-permute-start | bytes 393224 | tf_op jit(solution)/shard_map/ppermute | solution.py:24
  33.2 3.7 %collective-permute-start.30 = (bf16[1,2,128,256]{3,2,1,0:T(8,128)(2,1)S(1)}, bf16[1,2,128,256]{3,2,1,0:T(8,128)(2,1)S(1)}, u32[]{:S(2)}, u32[]{:S(2)}) collective-permute-start(bf16[1,2,128,256]{3,2,1,0:T(8,128)(2,1)S(1)} %collective-permute-done.26.refs_27_), channel_id=1, source_target_pairs={{0,8},{1,9},{2,10},{3,11},{4,12},{5,13},{6,14},{7,15},{8,0},{9,1},... | collective-permute-start | bytes 393224 | tf_op jit(solution)/shard_map/ppermute | solution.py:24
  33.2 3.7 %collective-permute-start.14 = (bf16[1,2,128,256]{3,2,1,0:T(8,128)(2,1)S(1)}, bf16[1,2,128,256]{3,2,1,0:T(8,128)(2,1)S(1)}, u32[]{:S(2)}, u32[]{:S(2)}) collective-permute-start(bf16[1,2,128,256]{3,2,1,0:T(8,128)(2,1)S(1)} %collective-permute-done.10.refs_10_), channel_id=1, source_target_pairs={{0,8},{1,9},{2,10},{3,11},{4,12},{5,13},{6,14},{7,15},{8,0},{9,1},... | collective-permute-start | bytes 393224 | tf_op jit(solution)/shard_map/ppermute | solution.py:24
  33.8 3.2 %collective-permute-start.13 = (bf16[1,2,128,256]{3,2,1,0:T(8,128)(2,1)S(1)}, bf16[1,2,128,256]{3,2,1,0:T(8,128)(2,1)S(1)}, u32[]{:S(2)}, u32[]{:S(2)}) collective-permute-start(bf16[1,2,128,256]{3,2,1,0:T(8,128)(2,1)S(1)} %collective-permute-done.9.refs_9_), channel_id=1, source_target_pairs={{0,8},{1,9},{2,10},{3,11},{4,12},{5,13},{6,14},{7,15},{8,0},{9,1},... | collective-permute-start | bytes 393224 | tf_op jit(solution)/shard_map/ppermute | solution.py:24
  36.9 1.3 %collective-permute-start.15 = (bf16[1,2,128,256]{3,2,1,0:T(8,128)(2,1)S(1)}, bf16[1,2,128,256]{3,2,1,0:T(8,128)(2,1)S(1)}, u32[]{:S(2)}, u32[]{:S(2)}) collective-permute-start(bf16[1,2,128,256]{3,2,1,0:T(8,128)(2,1)S(1)} %collective-permute-done.11.refs_11_), channel_id=1, source_target_pairs={{0,8},{1,9},{2,10},{3,11},{4,12},{5,13},{6,14},{7,15},{8,0},{9,1},... | collective-permute-start | bytes 393224 | tf_op jit(solution)/shard_map/ppermute | solution.py:24
  38.3 1.7 %copy-start = (bf16[3,1,1,48,64,128]{5,4,3,2,1,0:T(8,128)(2,1)S(1)}, bf16[3,1,1,48,64,128]{5,4,3,2,1,0:T(8,128)(2,1)}, u32[]{:S(2)}) copy-start(bf16[3,1,1,48,64,128]{5,4,3,2,1,0:T(8,128)(2,1)} %lmat_ref.1) | copy-start | bytes 7077892
  39.9 0.9 %copy-start.1 = (bf16[1,2,128,256]{3,2,1,0:T(8,128)(2,1)S(1)}, bf16[1,2,128,256]{3,2,1,0:T(8,128)(2,1)}, u32[]{:S(2)}) copy-start(bf16[1,2,128,256]{3,2,1,0:T(8,128)(2,1)} %refs_16_.1) | copy-start | bytes 393220
  40.8 0.7 copy-start.2
  41.5 0.7 copy-start.4
  42.2 0.7 copy-start.5
  42.9 12.2 %copy-start.3 = (s32[1,2,64]{2,1,0:T(2,128)S(1)}, s32[1,2,64]{2,1,0:T(2,128)}, u32[]{:S(2)}) copy-start(s32[1,2,64]{2,1,0:T(2,128)} %ex_ref.3) | copy-start | bytes 1540
  53.1 8.4 %collective-permute-start.31 = (bf16[4,256,128]{2,1,0:T(8,128)(2,1)S(1)}, bf16[4,256,128]{2,1,0:T(8,128)(2,1)S(1)}, u32[]{:S(2)}, u32[]{:S(2)}) collective-permute-start(bf16[4,256,128]{2,1,0:T(8,128)(2,1)S(1)} %get-tuple-element.14), channel_id=1, source_target_pairs={{0,1},{1,0},{2,3},{3,2},{4,5},{5,4},{6,7},{7,6},{8,9},{9,8},{10,11... | collective-permute-start | bytes 786440 | tf_op jit(solution)/shard_map/ppermute | solution.py:222
  53.7 9.0 %collective-permute-start.33 = (bf16[4,256,128]{2,1,0:T(8,128)(2,1)S(1)}, bf16[4,256,128]{2,1,0:T(8,128)(2,1)S(1)}, u32[]{:S(2)}, u32[]{:S(2)}) collective-permute-start(bf16[4,256,128]{2,1,0:T(8,128)(2,1)S(1)} %get-tuple-element.16), channel_id=1, source_target_pairs={{0,2},{1,3},{2,0},{3,1},{4,6},{5,7},{6,4},{7,5},{8,10},{9,11},{10,... | collective-permute-start | bytes 786440 | tf_op jit(solution)/shard_map/ppermute | solution.py:222
  61.6 5.0 %collective-permute-start.32 = (bf16[2,256,128]{2,1,0:T(8,128)(2,1)S(1)}, bf16[2,256,128]{2,1,0:T(8,128)(2,1)S(1)}, u32[]{:S(2)}, u32[]{:S(2)}) collective-permute-start(bf16[2,256,128]{2,1,0:T(8,128)(2,1)S(1)} %slice.48), channel_id=1, source_target_pairs={{0,2},{1,3},{2,0},{3,1},{4,6},{5,7},{6,4},{7,5},{8,10},{9,11},{10,... | collective-permute-start | bytes 393224 | tf_op jit(solution)/shard_map/ppermute | solution.py:222
  62.8 5.0 %collective-permute-start.34 = (bf16[2,256,128]{2,1,0:T(8,128)(2,1)S(1)}, bf16[2,256,128]{2,1,0:T(8,128)(2,1)S(1)}, u32[]{:S(2)}, u32[]{:S(2)}) collective-permute-start(bf16[2,256,128]{2,1,0:T(8,128)(2,1)S(1)} %slice.47), channel_id=1, source_target_pairs={{0,1},{1,0},{2,3},{3,2},{4,5},{5,4},{6,7},{7,6},{8,9},{9,8},{10,11... | collective-permute-start | bytes 393224 | tf_op jit(solution)/shard_map/ppermute | solution.py:222
  67.9 7.3 %collective-permute-start.35 = (bf16[1,512,128]{2,1,0:T(8,128)(2,1)S(1)}, bf16[1,512,128]{2,1,0:T(8,128)(2,1)S(1)}, u32[]{:S(2)}, u32[]{:S(2)}) collective-permute-start(bf16[1,512,128]{2,1,0:T(8,128)(2,1)S(1)} %fusion.3), channel_id=1, source_target_pairs={{0,4},{1,5},{2,6},{3,7},{4,0},{5,1},{6,2},{7,3},{8,12},{9,13},{10,... | collective-permute-start | bytes 393224 | tf_op jit(solution)/shard_map/ppermute | solution.py:222
